TPU v7x, 512 devices: a whole 4x8x8 slice. The times are simulated.
512 devices in a mesh: pipe: 8 (over x, core), expert: 64 (over y, z).
Axes of the slice: x: 4, y: 8, z: 8, core: 2. Of those that a mesh axis runs over, the one named last changes fastest.
Arguments:
- act_down: bfloat16 [8, 4096, 3584], P('pipe', 'expert'), may hold values from -6 to 6
- act_up: bfloat16 [8, 4096, 3584], P('pipe', 'expert'), may hold values from -6 to 6
- norm_gain: bfloat16 [8, 3584], P('pipe'), may hold values from 0.5 to 1.5
- gate_weight: bfloat16 [8, 8192, 3584], P('pipe', 'expert'), may hold values from -0.09375 to 0.09375
- up_weight: bfloat16 [8, 8192, 3584], P('pipe', 'expert'), may hold values from -0.09375 to 0.09375
- down_weight: bfloat16 [8, 1024, 28672], P('pipe', None, 'expert'), may hold values from -0.1875 to 0.1875
- routes_down: int32 [8, 4096, 1], P('pipe', 'expert'), may hold values from 0 to 7; in each aligned block of 64 rows (0 to 63, 64 to 127, ..., all dimensions but the last counted through in order) at most 10 rows name the same one
- gates_down: float32 [8, 4096, 1], P('pipe', 'expert'), may hold values from 0.5 to 2
- routes_up: int32 [8, 4096, 1], P('pipe', 'expert'), may hold values from 0 to 7; in each aligned block of 64 rows (0 to 63, 64 to 127, ..., all dimensions but the last counted through in order) at most 10 rows name the same one
- gates_up: float32 [8, 4096, 1], P('pipe', 'expert'), may hold values from 0.5 to 2
Outputs:
- out_down: bfloat16 [8, 4096, 3584], P('pipe', 'expert')
- out_up: bfloat16 [8, 4096, 3584], P('pipe', 'expert')
Inputs may be any that keep to these rules, and one draw needn't show every extreme that they name: `routes_down`: the 1 expert named by one token are all different. In the rows of one device (aligned blocks of 64 rows), no expert is named by more than 10 rows, a bound that some block reaches. `routes_up`: as for routes_down.
All inputs are finite; a program needn't handle non-finite values.
Results may differ from a plain program's by a relative error of at most 0.0055.
Values may be sent and summed in bfloat16 or wider, within the bound.
A program may use at most 128 MiB of HBM per device.

v0:
```python
import jax
import jax.numpy as jnp
from jax import lax
from jax.sharding import PartitionSpec as P

EXPERTS = 8
CAP = 10


EPSILON = 1e-06


def swapped(value, axis, apart):
    mask = 2**apart
    pairs = [(source, source ^ mask) for source in range(lax.axis_size(axis))]
    return lax.ppermute(value, axis, pairs)


def passed_along(shard, axis, by):
    count = lax.axis_size(axis)
    pairs = [(i, i + by) for i in range(count) if 0 <= i + by < count]
    return lax.ppermute(shard, axis, pairs)


def normalize(activations, norm_scale):
    widened = activations.astype(jnp.float32)
    inverse_rms = lax.rsqrt(jnp.mean(widened * widened, axis=-1, keepdims=True) + EPSILON)
    return (widened, (widened * inverse_rms * norm_scale.astype(jnp.float32)).astype(jnp.bfloat16))


def slot_tables(routes, gate_weights):
    expert_ids = jnp.arange(EXPERTS, dtype=jnp.int32)
    matches = routes[None, :, :] == expert_ids[:, None, None]
    chosen = jnp.any(matches, axis=2).astype(jnp.int32)
    earlier = jnp.cumsum(chosen, axis=1) - chosen
    slot_ids = jnp.arange(CAP, dtype=jnp.int32)
    picker = (chosen[:, None, :] == 1) & (earlier[:, None, :] == slot_ids[None, :, None])
    gate_sum = jnp.sum(jnp.where(matches, gate_weights[None, :, :], 0.0), axis=2)
    return (picker, picker.astype(jnp.float32) * gate_sum[:, None, :])


def expert_rows(received, gate_rows, up_rows, down_cols):
    flattened = received.reshape(-1, received.shape[-1])
    dims = (((1,), (1,)), ((), ()))
    gate_pre = lax.dot_general(flattened, gate_rows, dims, preferred_element_type=jnp.float32)
    up_pre = lax.dot_general(flattened, up_rows, dims, preferred_element_type=jnp.float32)
    gathered = (jax.nn.silu(gate_pre) * up_pre).astype(jnp.bfloat16)
    position = lax.axis_index("expert")
    group_size = lax.axis_size("expert") // EXPERTS
    for bit_number in range(group_size.bit_length() - 1):
        partner = swapped(gathered, "expert", bit_number)
        high_bit = position // 2**bit_number % 2 == 1
        gathered = jnp.where(
            high_bit,
            jnp.concatenate([partner, gathered], axis=1),
            jnp.concatenate([gathered, partner], axis=1),
        )
    columns = jnp.dot(gathered, down_cols, preferred_element_type=jnp.float32).astype(jnp.bfloat16)
    shaped = columns.reshape(received.shape[0], received.shape[1], columns.shape[-1])
    return lax.all_to_all(shaped, "expert", split_axis=0, concat_axis=0, tiled=True)


def apply_layer(activations, norm_scale, routes, gate_weights, gate_rows, up_rows, down_cols):
    widened, normed = normalize(activations, norm_scale)
    picker, weighted = slot_tables(routes, gate_weights)
    outgoing = jnp.einsum(
        "ect,td->ecd", picker.astype(jnp.bfloat16), normed, preferred_element_type=jnp.float32
    ).astype(jnp.bfloat16)
    expert_count = lax.axis_size("expert")
    group_size = expert_count // EXPERTS
    model_width = outgoing.shape[-1]
    part_width = model_width // group_size
    buffer = jnp.broadcast_to(outgoing[:, None], (EXPERTS, group_size, CAP, model_width)).reshape(
        expert_count, CAP, model_width
    )
    returned = expert_rows(
        lax.all_to_all(buffer, "expert", split_axis=0, concat_axis=0, tiled=True),
        gate_rows,
        up_rows,
        down_cols,
    )
    combined = (
        returned.reshape(EXPERTS, group_size, CAP, part_width)
        .transpose(0, 2, 1, 3)
        .reshape(EXPERTS, CAP, model_width)
        .astype(jnp.float32)
    )
    expert_sum = jnp.einsum("ect,ecd->td", weighted, combined, precision=lax.Precision.HIGHEST)
    return (widened + expert_sum).astype(jnp.bfloat16)


def body(
    act_down,
    act_up,
    norm_gain,
    gate_weight,
    up_weight,
    down_weight,
    routes_down,
    gates_down,
    routes_up,
    gates_up,
):
    norm_scale = norm_gain[0]
    gate_rows = gate_weight[0]
    up_rows = up_weight[0]
    down_cols = down_weight[0]
    first_down = apply_layer(
        act_down[0], norm_scale, routes_down[0], gates_down[0], gate_rows, up_rows, down_cols
    )
    first_up = apply_layer(
        act_up[0], norm_scale, routes_up[0], gates_up[0], gate_rows, up_rows, down_cols
    )
    section_index = lax.axis_index("pipe")
    section_count = lax.axis_size("pipe")
    from_above = passed_along(first_down, "pipe", 1)
    from_below = passed_along(first_up, "pipe", -1)
    out_down = jnp.where(section_index == 0, first_up, from_above)
    out_up = jnp.where(section_index == section_count - 1, first_down, from_below)
    return (out_down[None], out_up[None])


def solution(mesh):
    return jax.shard_map(
        body,
        mesh=mesh,
        in_specs=(
            P("pipe", "expert", None),
            P("pipe", "expert", None),
            P("pipe", None),
            P("pipe", "expert", None),
            P("pipe", "expert", None),
            P("pipe", None, "expert"),
            P("pipe", "expert", None),
            P("pipe", "expert", None),
            P("pipe", "expert", None),
            P("pipe", "expert", None),
        ),
        out_specs=(P("pipe", "expert", None), P("pipe", "expert", None)),
        check_vma=False,
    )
```

profile of v0, /device:TPU:1, one launch (start us, length us, event | category | flops | bytes accessed | tf_op | source)
XLA Modules:
  0.0 768.2 jit_solution(12352192934824199570)
XLA Ops:
  0.6 0.0 copy-start
  0.6 0.8 convert_reduce_fusion
  1.5 0.7 fusion.69
  2.1 0.2 reduce_window_sum.17
  2.4 0.7 fusion.68
  3.0 1.2 fusion.18
  4.2 1.5 convolution_convert_fusion.1
  5.7 3.8 broadcast_in_dim.57
  9.6 17.5 %all-to-all-start = ((bf16[64,10,3584]{2,1,0:T(8,128)(2,1)}), bf16[64,10,3584]{2,1,0:T(8,128)(2,1)}, u32[]{:S(2)}, u32[]{:S(2)}) async-start(bf16[64,10,3584]{2,1,0:T(8,128)(2,1)} %bitcast.80), calls=%async_computation | async-start | bytes 14680064 | tf_op jit(solution)/shard_map/all_to_all | solution.py:77
  27.1 0.2 reduce_window_sum.18
  27.3 0.2 fusion.21
  27.5 0.5 convolution_convert_fusion
  28.0 216.4 %all-to-all-done = bf16[64,10,3584]{2,1,0:T(8,128)(2,1)} async-done(((bf16[64,10,3584]{2,1,0:T(8,128)(2,1)}), bf16[64,10,3584]{2,1,0:T(8,128)(2,1)}, u32[]{:S(2)}, u32[]{:S(2)}) %all-to-all-start) | async-done | bytes 4587552 | tf_op jit(solution)/shard_map/all_to_all | solution.py:77
  244.5 3.9 broadcast_in_dim.60
  248.3 38.3 %all-to-all-start.2 = ((bf16[64,10,3584]{2,1,0:T(8,128)(2,1)}), bf16[64,10,3584]{2,1,0:T(8,128)(2,1)}, u32[]{:S(2)}, u32[]{:S(2)}) async-start(bf16[64,10,3584]{2,1,0:T(8,128)(2,1)} %bitcast.79), calls=%async_computation.2 | async-start | bytes 14680064 | tf_op jit(solution)/shard_map/all_to_all | solution.py:77
  286.6 0.0 copy-start.9
  286.7 8.0 %reshape.287 = bf16[640,3584]{1,0:T(8,128)(2,1)} reshape(bf16[64,10,3584]{2,1,0:T(8,128)(2,1)} %all-to-all-done) | data formatting | bytes 9175040 | tf_op jit(solution)/shard_map/reshape | solution.py:43
  294.7 4.0 fusion.30
  298.7 1.5 fusion.16
  300.2 2.9 collective-permute-start
  303.1 194.9 %all-to-all-done.2 = bf16[64,10,3584]{2,1,0:T(8,128)(2,1)} async-done(((bf16[64,10,3584]{2,1,0:T(8,128)(2,1)}), bf16[64,10,3584]{2,1,0:T(8,128)(2,1)}, u32[]{:S(2)}, u32[]{:S(2)}) %all-to-all-start.2) | async-done | bytes 4587552 | tf_op jit(solution)/shard_map/all_to_all | solution.py:77
  498.0 8.0 %reshape.292 = bf16[640,3584]{1,0:T(8,128)(2,1)} reshape(bf16[64,10,3584]{2,1,0:T(8,128)(2,1)} %all-to-all-done.2) | data formatting | bytes 9175040 | tf_op jit(solution)/shard_map/reshape | solution.py:43
  506.0 0.0 collective-permute-done
  506.0 0.1 maximum_select_fusion.6
  506.1 0.0 slice-start.1
  506.1 7.7 collective-permute-start.1
  513.7 3.8 fusion.28
  517.5 0.6 collective-permute-done.1
  518.2 0.2 maximum_select_fusion.4
  518.4 16.9 %collective-permute-start.2 = (bf16[640,512]{0,1:T(8,128)(2,1)S(1)}, bf16[640,512]{0,1:T(8,128)(2,1)}, u32[]{:S(2)}, u32[]{:S(2)}) collective-permute-start(bf16[640,512]{0,1:T(8,128)(2,1)S(1)} %maximum_select_fusion.4), channel_id=1, source_target_pairs={{0,4},{1,5},{2,6},{3,7},{4,0},{5,1},{6,2},{7,3},{8,12},{9,13},{10,... | collective-permute-start | bytes 1966088 | tf_op jit(solution)/shard_map/ppermute | solution.py:16
  535.4 1.5 fusion.17
  536.9 1.9 collective-permute-start.3
  538.9 23.4 %collective-permute-done.3 = bf16[640,128]{0,1:T(8,128)(2,1)S(1)} collective-permute-done((bf16[640,128]{0,1:T(8,128)(2,1)S(1)}, bf16[640,128]{0,1:T(8,128)(2,1)S(1)}, u32[]{:S(2)}, u32[]{:S(2)}) %collective-permute-start.3) | collective-permute-done | bytes 163872 | tf_op jit(solution)/shard_map/ppermute | solution.py:16
  562.3 0.1 maximum_select_fusion.7
  562.4 1.9 collective-permute-start.4
  564.3 0.0 collective-permute-done.2
  564.3 2.2 convolution_convert_fusion.3
  566.5 0.3 copy.14
  566.8 1.3 reshape.288
  568.1 62.1 %all-to-all-start.1 = ((bf16[64,10,448]{2,1,0:T(8,128)(2,1)}), bf16[64,10,448]{2,1,0:T(8,128)(2,1)S(1)}, u32[]{:S(2)}, u32[]{:S(2)}) async-start(bf16[64,10,448]{2,1,0:T(8,128)(2,1)} %reshape.288), calls=%async_computation.1 | async-start | bytes 2097152 | tf_op jit(solution)/shard_map/all_to_all | solution.py:60
  630.1 0.0 collective-permute-done.4
  630.1 0.2 maximum_select_fusion.5
  630.4 7.0 collective-permute-start.5
  637.4 44.0 %collective-permute-done.5 = bf16[640,512]{0,1:T(8,128)(2,1)S(1)} collective-permute-done((bf16[640,512]{0,1:T(8,128)(2,1)S(1)}, bf16[640,512]{0,1:T(8,128)(2,1)S(1)}, u32[]{:S(2)}, u32[]{:S(2)}) %collective-permute-start.5) | collective-permute-done | bytes 655392 | tf_op jit(solution)/shard_map/ppermute | solution.py:16
  681.4 0.9 convolution_convert_fusion.2
  682.4 0.3 copy.17
  682.6 0.0 copy-start.5
  682.6 0.0 copy-start.7
  682.6 1.3 reshape.293
  683.9 0.0 all-to-all-done.1
  683.9 12.8 %all-to-all-start.3 = ((bf16[64,10,448]{2,1,0:T(8,128)(2,1)}), bf16[64,10,448]{2,1,0:T(8,128)(2,1)S(1)}, u32[]{:S(2)}, u32[]{:S(2)}) async-start(bf16[64,10,448]{2,1,0:T(8,128)(2,1)} %reshape.293), calls=%async_computation.3 | async-start | bytes 2097152 | tf_op jit(solution)/shard_map/all_to_all | solution.py:60
  696.7 0.0 copy-start.2
  696.8 1.3 copy.27
  698.0 1.8 reshape.290
  699.9 1.4 fusion.2
  701.3 3.2 collective-permute-start.7
  704.6 18.7 %all-to-all-done.3 = bf16[64,10,448]{2,1,0:T(8,128)(2,1)S(1)} async-done(((bf16[64,10,448]{2,1,0:T(8,128)(2,1)}), bf16[64,10,448]{2,1,0:T(8,128)(2,1)S(1)}, u32[]{:S(2)}, u32[]{:S(2)}) %all-to-all-start.3) | async-done | bytes 573472 | tf_op jit(solution)/shard_map/all_to_all | solution.py:60
  723.2 1.2 copy.26
  724.4 1.8 reshape.295
  726.3 0.6 fusion.3
  726.9 35.0 %collective-permute-start.6 = (bf16[64,3584]{1,0:T(8,128)(2,1)S(1)}, bf16[64,3584]{1,0:T(8,128)(2,1)S(1)}, u32[]{:S(2)}, u32[]{:S(2)}) collective-permute-start(bf16[64,3584]{1,0:T(8,128)(2,1)S(1)} %fusion.3), channel_id=1, source_target_pairs={{0,64},{64,128},{128,192},{192,256},{256,320},{320,384},{384,448},... | collective-permute-start | bytes 1376264 | tf_op jit(solution)/shard_map/ppermute | solution.py:22
  762.0 0.8 select_bitcast_fusion
  762.8 4.6 collective-permute-done.6
  767.3 0.8 select_bitcast_fusion.1
  (28 shorter events, 0.1 us)
Async XLA Ops:
  0.6 563.7 %copy-start = (bf16[1,1024,448]{1,2,0:T(8,128)(2,1)S(1)}, bf16[1,1024,448]{1,2,0:T(8,128)(2,1)}, u32[]{:S(2)}) copy-start(bf16[1,1024,448]{1,2,0:T(8,128)(2,1)} %param.15) | copy-start | bytes 2752516
  9.6 17.5 %copy-start.6 = (s32[1,64,1]{1,2,0:T(1,128)S(1)}, s32[1,64,1]{1,2,0:T(1,128)}, u32[]{:S(2)}) copy-start(s32[1,64,1]{1,2,0:T(1,128)} %param.16) | copy-start | bytes 772
  9.6 17.8 %copy-start.3 = (bf16[1,64,3584]{2,1,0:T(8,128)(2,1)S(1)}, bf16[1,64,3584]{2,1,0:T(8,128)(2,1)}, u32[]{:S(2)}) copy-start(bf16[1,64,3584]{2,1,0:T(8,128)(2,1)} %param.10) | copy-start | bytes 1376260
  9.6 234.9 %all-to-all-start = ((bf16[64,10,3584]{2,1,0:T(8,128)(2,1)}), bf16[64,10,3584]{2,1,0:T(8,128)(2,1)}, u32[]{:S(2)}, u32[]{:S(2)}) async-start(bf16[64,10,3584]{2,1,0:T(8,128)(2,1)} %bitcast.80), calls=%async_computation | async-start | bytes 14680064 | tf_op jit(solution)/shard_map/all_to_all | solution.py:77
  248.3 249.7 %all-to-all-start.2 = ((bf16[64,10,3584]{2,1,0:T(8,128)(2,1)}), bf16[64,10,3584]{2,1,0:T(8,128)(2,1)}, u32[]{:S(2)}, u32[]{:S(2)}) async-start(bf16[64,10,3584]{2,1,0:T(8,128)(2,1)} %bitcast.79), calls=%async_computation.2 | async-start | bytes 14680064 | tf_op jit(solution)/shard_map/all_to_all | solution.py:77
  286.6 8.0 %copy-start.9 = (bf16[1,128,3584]{2,1,0:T(8,128)(2,1)S(1)}, bf16[1,128,3584]{2,1,0:T(8,128)(2,1)}, u32[]{:S(2)}) copy-start(bf16[1,128,3584]{2,1,0:T(8,128)(2,1)} %param.13) | copy-start | bytes 2752516
  294.7 4.0 copy-start.1
  294.7 4.0 copy-start.10
  300.2 205.8 %collective-permute-start = (bf16[640,128]{0,1:T(8,128)(2,1)S(1)}, bf16[640,128]{0,1:T(8,128)(2,1)S(1)}, u32[]{:S(2)}, u32[]{:S(2)}) collective-permute-start(bf16[640,128]{0,1:T(8,128)(2,1)S(1)} %fusion.16), channel_id=1, source_target_pairs={{0,1},{1,0},{2,3},{3,2},{4,5},{5,4},{6,7},{7,6},{8,9},{9,8},{10,11... | collective-permute-start | bytes 491528 | tf_op jit(solution)/shard_map/ppermute | solution.py:16
  506.0 29.4 %slice-start = ((s8[4587520]{0:T(1024)(128)(4,1)}), s8[4194304]{0:T(1024)(128)(4,1)S(1)}, s32[]{:S(2)}) async-start(s8[4587520]{0:T(1024)(128)(4,1)} %bitcast.81), calls=%async_computation.4 | async-start | bytes 8388608
  506.1 29.3 %slice-start.1 = ((s8[4587520]{0:T(1024)(128)(4,1)}), s8[393216]{0:T(1024)(128)(4,1)S(1)}, s32[]{:S(2)}) async-start(s8[4587520]{0:T(1024)(128)(4,1)} %bitcast.81), calls=%async_computation.5 | async-start | bytes 786432
  506.1 12.1 %collective-permute-start.1 = (bf16[640,256]{0,1:T(8,128)(2,1)S(1)}, bf16[640,256]{0,1:T(8,128)(2,1)S(1)}, u32[]{:S(2)}, u32[]{:S(2)}) collective-permute-start(bf16[640,256]{0,1:T(8,128)(2,1)S(1)} %maximum_select_fusion.6), channel_id=1, source_target_pairs={{0,2},{1,3},{2,0},{3,1},{4,6},{5,7},{6,4},{7,5},{8,10},{9,11},{10,... | collective-permute-start | bytes 983048 | tf_op jit(solution)/shard_map/ppermute | solution.py:16
  518.4 45.9 %collective-permute-start.2 = (bf16[640,512]{0,1:T(8,128)(2,1)S(1)}, bf16[640,512]{0,1:T(8,128)(2,1)}, u32[]{:S(2)}, u32[]{:S(2)}) collective-permute-start(bf16[640,512]{0,1:T(8,128)(2,1)S(1)} %maximum_select_fusion.4), channel_id=1, source_target_pairs={{0,4},{1,5},{2,6},{3,7},{4,0},{5,1},{6,2},{7,3},{8,12},{9,13},{10,... | collective-permute-start | bytes 1966088 | tf_op jit(solution)/shard_map/ppermute | solution.py:16
  536.9 25.4 %collective-permute-start.3 = (bf16[640,128]{0,1:T(8,128)(2,1)S(1)}, bf16[640,128]{0,1:T(8,128)(2,1)S(1)}, u32[]{:S(2)}, u32[]{:S(2)}) collective-permute-start(bf16[640,128]{0,1:T(8,128)(2,1)S(1)} %fusion.17), channel_id=1, source_target_pairs={{0,1},{1,0},{2,3},{3,2},{4,5},{5,4},{6,7},{7,6},{8,9},{9,8},{10,11... | collective-permute-start | bytes 491528 | tf_op jit(solution)/shard_map/ppermute | solution.py:16
  562.4 67.7 %collective-permute-start.4 = (bf16[640,256]{0,1:T(8,128)(2,1)S(1)}, bf16[640,256]{0,1:T(8,128)(2,1)S(1)}, u32[]{:S(2)}, u32[]{:S(2)}) collective-permute-start(bf16[640,256]{0,1:T(8,128)(2,1)S(1)} %maximum_select_fusion.7), channel_id=1, source_target_pairs={{0,2},{1,3},{2,0},{3,1},{4,6},{5,7},{6,4},{7,5},{8,10},{9,11},{10,... | collective-permute-start | bytes 983048 | tf_op jit(solution)/shard_map/ppermute | solution.py:16
  568.1 115.8 %all-to-all-start.1 = ((bf16[64,10,448]{2,1,0:T(8,128)(2,1)}), bf16[64,10,448]{2,1,0:T(8,128)(2,1)S(1)}, u32[]{:S(2)}, u32[]{:S(2)}) async-start(bf16[64,10,448]{2,1,0:T(8,128)(2,1)} %reshape.288), calls=%async_computation.1 | async-start | bytes 2097152 | tf_op jit(solution)/shard_map/all_to_all | solution.py:60
  630.4 51.1 %collective-permute-start.5 = (bf16[640,512]{0,1:T(8,128)(2,1)S(1)}, bf16[640,512]{0,1:T(8,128)(2,1)S(1)}, u32[]{:S(2)}, u32[]{:S(2)}) collective-permute-start(bf16[640,512]{0,1:T(8,128)(2,1)S(1)} %maximum_select_fusion.5), channel_id=1, source_target_pairs={{0,4},{1,5},{2,6},{3,7},{4,0},{5,1},{6,2},{7,3},{8,12},{9,13},{10,... | collective-permute-start | bytes 1966088 | tf_op jit(solution)/shard_map/ppermute | solution.py:16
  682.6 14.1 %copy-start.5 = (s32[1,64,1]{1,2,0:T(1,128)S(1)}, s32[1,64,1]{1,2,0:T(1,128)}, u32[]{:S(2)}) copy-start(s32[1,64,1]{1,2,0:T(1,128)} %param.18) | copy-start | bytes 772
  682.6 14.1 %copy-start.7 = (f32[1,64,1]{1,2,0:T(1,128)S(1)}, f32[1,64,1]{1,2,0:T(1,128)}, u32[]{:S(2)}) copy-start(f32[1,64,1]{1,2,0:T(1,128)} %param.19) | copy-start | bytes 772
  683.9 39.3 %all-to-all-start.3 = ((bf16[64,10,448]{2,1,0:T(8,128)(2,1)}), bf16[64,10,448]{2,1,0:T(8,128)(2,1)S(1)}, u32[]{:S(2)}, u32[]{:S(2)}) async-start(bf16[64,10,448]{2,1,0:T(8,128)(2,1)} %reshape.293), calls=%async_computation.3 | async-start | bytes 2097152 | tf_op jit(solution)/shard_map/all_to_all | solution.py:60
  696.7 3.2 copy-start.2
  698.0 6.5 copy-start.8
  701.3 25.0 %copy-start.4 = (bf16[1,64,3584]{2,1,0:T(8,128)(2,1)S(1)}, bf16[1,64,3584]{2,1,0:T(8,128)(2,1)}, u32[]{:S(2)}) copy-start(bf16[1,64,3584]{2,1,0:T(8,128)(2,1)} %param.10) | copy-start | bytes 1376260
  701.3 60.7 %collective-permute-start.7 = (bf16[64,3584]{1,0:T(8,128)(2,1)}, bf16[64,3584]{1,0:T(8,128)(2,1)S(1)}, u32[]{:S(2)}, u32[]{:S(2)}) collective-permute-start(bf16[64,3584]{1,0:T(8,128)(2,1)} %fusion.2), channel_id=1, source_target_pairs={{64,0},{128,64},{192,128},{256,192},{320,256},{384,320},{448,384},... | collective-permute-start | bytes 1376264 | tf_op jit(solution)/shard_map/ppermute | solution.py:22
  726.9 40.4 %collective-permute-start.6 = (bf16[64,3584]{1,0:T(8,128)(2,1)S(1)}, bf16[64,3584]{1,0:T(8,128)(2,1)S(1)}, u32[]{:S(2)}, u32[]{:S(2)}) collective-permute-start(bf16[64,3584]{1,0:T(8,128)(2,1)S(1)} %fusion.3), channel_id=1, source_target_pairs={{0,64},{64,128},{128,192},{192,256},{256,320},{320,384},{384,448},... | collective-permute-start | bytes 1376264 | tf_op jit(solution)/shard_map/ppermute | solution.py:22
where the time goes:
time: 770 us; the launch traced here: 768 us
  waiting for transfers between devices  503 us (65%)
  starting transfers between devices  207 us (27%)
  local copies, waits for them, and re-layouts  32.9 us (4%)
  matrix products  17.9 us (2%)
    all_to_all x2, waiting for transfers between devices, apply_layer(): lax.all_to_all(buffer, 'expert', split_axis=0, concat_axis=0, tiled=True)  411 us
    all_to_all x2, starting transfers between devices, expert_rows(): lax.all_to_all(shaped, 'expert', split_axis=0, concat_axis=0, tiled=True)  74.8 us
    ppermute x6, waiting for transfers between devices, swapped(): return lax.ppermute(value, axis, pairs)  68.1 us
    all_to_all x2, starting transfers between devices, apply_layer(): lax.all_to_all(buffer, 'expert', split_axis=0, concat_axis=0, tiled=True)  55.8 us
    ppermute x6, starting transfers between devices, swapped(): return lax.ppermute(value, axis, pairs)  38.3 us
    ppermute x2, starting transfers between devices, passed_along(): return lax.ppermute(shard, axis, pairs)  38.3 us
    all_to_all x2, waiting for transfers between devices, expert_rows(): lax.all_to_all(shaped, 'expert', split_axis=0, concat_axis=0, tiled=True)  18.7 us
    reshape x2, local copies, waits for them, and re-layouts, expert_rows(): flattened = received.reshape(-1, received.shape[-1])  16 us
  transfers between devices with their start and end apart: 12, of which 7 were waited for; matrix products, arithmetic and copies ran while one was open for 6% of the time, Pallas kernels for 0%

commit v1 on v0

v1 whole, which is shorter than its diff:
```python
import functools

import jax
import jax.numpy as jnp
from jax import lax
from jax.experimental import pallas as pl
from jax.experimental.pallas import tpu as pltpu
from jax.sharding import PartitionSpec as P

EXPERTS = 8
CAP = 10
SLAB = 16
CHUNKS = 4
EPSILON = 1e-06

MESH = pl.DeviceIdType.MESH
F32 = jnp.float32
BF16 = jnp.bfloat16


def one_hot(condition):
    return jnp.where(condition, 1.0, 0.0).astype(BF16)


def iota(shape, dimension):
    return lax.broadcasted_iota(jnp.int32, shape, dimension)


def kernel(
    experts,
    sections,
    x_down,
    x_up,
    gain,
    gate_w,
    up_w,
    down_w,
    route_rows,
    route_cols_down,
    route_cols_up,
    gate_cols_down,
    gate_cols_up,
    out_down,
    out_up,
    gate_up,
    normed,
    slabs,
    landed,
    tokens,
    hidden_own,
    hidden,
    columns,
    returned,
    spread,
    final,
    residual,
    mixing,
    mixing_here,
    slab_send,
    slab_recv,
    token_send,
    token_recv,
    hidden_send,
    hidden_recv,
    hidden_copy,
    columns_send,
    columns_recv,
    final_send,
    final_send_same,
    final_recv,
    residual_send,
    residual_recv,
    mixing_send,
    mixing_recv,
):
    ring = tokens.shape[2]
    rows = experts * CAP
    slots = experts * SLAB
    count, depth = x_down.shape
    width = depth // CHUNKS
    units = gate_w.shape[0]
    pipe = lax.axis_index("pipe")
    position = lax.axis_index("expert")
    y = position // ring
    z = position % ring
    x_refs = (x_down, x_up)
    route_cols = (route_cols_down, route_cols_up)
    gate_cols = (gate_cols_down, gate_cols_up)
    outs = (out_down, out_up)

    def at_y(k):
        return (pipe, lax.rem(y + k, experts) * ring + z)

    def at_z(k):
        return (pipe, y * ring + lax.rem(z + k, ring))

    barrier = pltpu.get_barrier_semaphore()

    def greet(device):
        pl.semaphore_signal(barrier, inc=1, device_id=device, device_id_type=MESH)

    @pl.loop(1, experts)
    def _(k):
        greet(at_y(k))

    @pl.loop(1, ring)
    def _(k):
        greet(at_z(k))

    @pl.when(pipe > 0)
    def _():
        @pl.loop(0, experts)
        def _(k):
            greet((pipe - 1, k * ring + z))

    @pl.when(pipe < sections - 1)
    def _():
        @pl.loop(0, experts)
        def _(k):
            greet((pipe + 1, k * ring + z))

    neighbours = jnp.where(pipe > 0, 1, 0) + jnp.where(pipe < sections - 1, 1, 0)
    greeted = experts - 1 + ring - 1 + experts * neighbours

    def wait(ref, sem):
        pltpu.make_async_copy(ref, ref, sem).wait()

    def normalize(g):
        x_ref = x_refs[g]
        total = jnp.zeros((count, 1), F32)
        for c in range(CHUNKS):
            part = x_ref[:, c * width : (c + 1) * width].astype(F32)
            total = total + jnp.sum(part * part, axis=-1, keepdims=True)
        inverse = lax.rsqrt(total / depth + EPSILON)
        for c in range(CHUNKS):
            cut = slice(c * width, (c + 1) * width)
            part = x_ref[:, cut].astype(F32)
            normed[g, :, cut] = (part * inverse * gain[:, cut].astype(F32)).astype(BF16)

    def pick(g):
        slot = iota((slots, count), 0)
        named = one_hot(route_rows[g : g + 1, :] == slot // SLAB)
        earlier = one_hot(iota((count, count), 0) < iota((count, count), 1))
        rank = jnp.dot(named, earlier, preferred_element_type=F32)
        same = rank == (slot % SLAB).astype(F32)
        return jnp.where(same, named.astype(F32), 0.0).astype(BF16)

    def mix(g):
        slot = iota((count, slots), 1)
        named = one_hot(route_cols[g][...] == slot // SLAB)
        earlier = one_hot(iota((count, count), 1) < iota((count, count), 0))
        rank = jnp.dot(earlier, named, preferred_element_type=F32)
        same = rank == (slot % SLAB).astype(F32)
        mixing[g] = jnp.where(same, named.astype(F32), 0.0) * gate_cols[g][...]

    def slab(k):
        return pl.ds(pl.multiple_of(k * SLAB, SLAB), SLAB)

    def dispatch(g, c, picker):
        cut = slice(c * width, (c + 1) * width)
        slabs[g, c] = jnp.dot(
            picker, normed[g, :, cut], preferred_element_type=F32
        ).astype(BF16)
        pltpu.make_async_copy(
            slabs.at[g, c, slab(y)], landed.at[g, c, slab(y)], slab_recv.at[g, c]
        ).start()

        @pl.loop(1, experts)
        def _(k):
            pltpu.make_async_remote_copy(
                src_ref=slabs.at[g, c, slab(lax.rem(y + k, experts))],
                dst_ref=landed.at[g, c, slab(y)],
                send_sem=slab_send.at[g, c],
                recv_sem=slab_recv.at[g, c],
                device_id=at_y(k),
                device_id_type=MESH,
            ).start()

    def last(g):
        return pipe == (sections - 1 if g == 0 else 0)

    def onward(g):
        return pipe + 1 if g == 0 else pipe - 1

    def send_residual(g):
        pairs = (
            (x_refs[g], residual, residual_send, residual_recv),
            (mixing.at[g], mixing_here, mixing_send, mixing_recv),
        )

        @pl.when(last(g))
        def _():
            for source, target, _, sem in pairs:
                pltpu.make_async_copy(source, target.at[1 - g], sem.at[1 - g]).start()

        @pl.when(jnp.logical_not(last(g)))
        def _():
            for source, target, sent, sem in pairs:
                pltpu.make_async_remote_copy(
                    src_ref=source,
                    dst_ref=target.at[g],
                    send_sem=sent.at[g],
                    recv_sem=sem.at[g],
                    device_id=(onward(g), position),
                    device_id_type=MESH,
                ).start()

    def hops(direction, part):
        return ring // 2 if direction == part % 2 else ring - 1 - ring // 2

    def behind(direction, k):
        return lax.rem(z + (ring - k if direction == 0 else k), ring)

    def ahead(direction):
        return at_z(1 if direction == 0 else ring - 1)

    def token_copy(g, direction, c, hop):
        block = tokens.at[g, c, behind(direction, hop)]
        return pltpu.make_async_remote_copy(
            src_ref=block,
            dst_ref=block,
            send_sem=token_send.at[g, direction, c, hop],
            recv_sem=token_recv.at[g, direction, c, hop],
            device_id=ahead(direction),
            device_id_type=MESH,
        )

    def compact(g, c):
        wait(landed.at[g, c], slab_recv.at[g, c])
        slot, row = iota((rows, slots), 1), iota((rows, slots), 0)
        inside = slot % SLAB
        keep = one_hot((row == slot // SLAB * CAP + inside) & (inside < CAP))
        tokens[g, c, z] = jnp.dot(
            keep, landed[g, c], preferred_element_type=F32
        ).astype(BF16)
        for direction in range(2):
            if hops(direction, c):
                token_copy(g, direction, c, 0).start()

    def token_stage(g, stage):
        for c in range(CHUNKS):
            for direction in range(2):
                if stage <= hops(direction, c):
                    wait(
                        tokens.at[g, c, behind(direction, stage)],
                        token_recv.at[g, direction, c, stage - 1],
                    )
                if stage < hops(direction, c):
                    token_copy(g, direction, c, stage).start()

    def hide(g, blocks):
        total = jnp.zeros((len(blocks) * rows, 2 * units), F32)
        for c in range(CHUNKS):
            parts = [tokens[g, c, block] for block in blocks]
            part = parts[0] if len(parts) == 1 else jnp.concatenate(parts, axis=0)
            total = total + lax.dot_general(
                part,
                gate_up[:, c * width : (c + 1) * width],
                (((1,), (1,)), ((), ())),
                preferred_element_type=F32,
            )
        units_out = (jax.nn.silu(total[:, :units]) * total[:, units:]).astype(BF16)
        for i, block in enumerate(blocks):
            start = pl.multiple_of(block * rows, 16)
            hidden_own[g, pl.ds(start, rows), :] = units_out[i * rows : (i + 1) * rows]

    def hide_stage(g, stage):
        if stage == 0:
            hide(g, [z])
        elif 2 * stage == ring:
            hide(g, [behind(0, stage)])
        else:
            hide(g, [behind(0, stage), behind(1, stage)])

    half_rows = ring * rows // 2

    def hidden_part(g, half, owner):
        lanes = pl.ds(pl.multiple_of(owner * units, units), units)
        return hidden.at[g, pl.ds(half * half_rows, half_rows), lanes]

    def hidden_copy_own(g):
        lanes = pl.ds(pl.multiple_of(z * units, units), units)
        return pltpu.make_async_copy(
            hidden_own.at[g], hidden.at[g, :, lanes], hidden_copy.at[g]
        )

    def hidden_ring(g, direction, half, hop):
        if hop == 0:
            source = hidden_own.at[g, pl.ds(half * half_rows, half_rows)]
        else:
            source = hidden_part(g, half, behind(direction, hop))
        return pltpu.make_async_remote_copy(
            src_ref=source,
            dst_ref=hidden_part(g, half, behind(direction, hop)),
            send_sem=hidden_send.at[g, direction, half, hop],
            recv_sem=hidden_recv.at[g, direction, half, hop],
            device_id=ahead(direction),
            device_id_type=MESH,
        )

    def hidden_stage(g, stage):
        for half in range(2):
            for direction in range(2):
                if 1 <= stage <= hops(direction, half):
                    wait(
                        hidden_part(g, half, behind(direction, stage)),
                        hidden_recv.at[g, direction, half, stage - 1],
                    )
                if stage < hops(direction, half):
                    hidden_ring(g, direction, half, stage).start()

    def project(g):
        hidden_copy_own(g).wait()
        for half in range(2):
            blocks = ring // 2
            result = jnp.dot(
                hidden[g, half * half_rows : (half + 1) * half_rows, :],
                down_w[...],
                preferred_element_type=F32,
            ).astype(BF16)
            for i in range(blocks):
                columns[g, half * blocks + i] = result[i * rows : (i + 1) * rows]
        pltpu.make_async_copy(
            columns.at[g, z], returned.at[g, z], columns_recv.at[g]
        ).start()

        @pl.loop(1, ring)
        def _(k):
            pltpu.make_async_remote_copy(
                src_ref=columns.at[g, lax.rem(z + k, ring)],
                dst_ref=returned.at[g, z],
                send_sem=columns_send.at[g],
                recv_sem=columns_recv.at[g],
                device_id=at_z(k),
                device_id_type=MESH,
            ).start()

    def give_back(g):
        wait(returned.at[g], columns_recv.at[g])
        slot, row = iota((slots, rows), 0), iota((slots, rows), 1)
        inside = slot % SLAB
        keep = one_hot((row == slot // SLAB * CAP + inside) & (inside < CAP))
        for k in range(ring // 2):
            parts = [
                jnp.dot(keep, returned[g, 2 * k + i], preferred_element_type=F32)
                for i in range(2)
            ]
            spread[g, k] = jnp.concatenate(parts, axis=1).astype(BF16)

        @pl.when(last(g))
        def _():
            pltpu.make_async_copy(
                spread.at[g, :, slab(y)], final.at[1 - g, :, slab(y)], final_recv.at[1 - g]
            ).start()

            @pl.loop(1, experts)
            def _(k):
                pltpu.make_async_remote_copy(
                    src_ref=spread.at[g, :, slab(lax.rem(y + k, experts))],
                    dst_ref=final.at[1 - g, :, slab(y)],
                    send_sem=final_send.at[g],
                    recv_sem=final_recv.at[1 - g],
                    device_id=at_y(k),
                    device_id_type=MESH,
                ).start()

        @pl.when(jnp.logical_not(last(g)))
        def _():
            pltpu.make_async_remote_copy(
                src_ref=spread.at[g, :, slab(y)],
                dst_ref=final.at[g, :, slab(y)],
                send_sem=final_send_same.at[g],
                recv_sem=final_recv.at[g],
                device_id=(onward(g), position),
                device_id_type=MESH,
            ).start()

            @pl.loop(1, experts)
            def _(k):
                target = lax.rem(y + k, experts)
                pltpu.make_async_remote_copy(
                    src_ref=spread.at[g, :, slab(target)],
                    dst_ref=final.at[g, :, slab(y)],
                    send_sem=final_send.at[g],
                    recv_sem=final_recv.at[g],
                    device_id=(onward(g), target * ring + z),
                    device_id_type=MESH,
                ).start()

    def combine(o):
        wait(residual.at[o], residual_recv.at[o])
        wait(mixing_here.at[o], mixing_recv.at[o])
        wait(final.at[o], final_recv.at[o])
        weights = mixing_here[o]
        picker = one_hot(weights != 0.0)
        weight = jnp.sum(weights, axis=-1, keepdims=True)
        span = final.shape[-1]
        for k in range(final.shape[1]):
            cut = slice(k * span, (k + 1) * span)
            picked = jnp.dot(picker, final[o, k], preferred_element_type=F32)
            outs[o][:, cut] = (residual[o, :, cut].astype(F32) + weight * picked).astype(BF16)

    normalize(0)
    picker = pick(0)
    mix(0)
    pl.semaphore_wait(barrier, greeted)
    for c in range(CHUNKS):
        dispatch(0, c, picker)
    normalize(1)
    picker = pick(1)
    mix(1)
    for c in range(CHUNKS):
        dispatch(1, c, picker)
    for g in range(2):
        send_residual(g)
    gate_up[:units] = gate_w[...]
    gate_up[units:] = up_w[...]

    for c in range(CHUNKS):
        compact(0, c)
    hide_stage(0, 0)
    final_stage = ring // 2
    for stage in range(1, final_stage):
        token_stage(0, stage)
        hide_stage(0, stage)
    for c in range(CHUNKS):
        compact(1, c)
    token_stage(0, final_stage)
    hide_stage(0, final_stage)
    hidden_copy_own(0).start()
    hidden_stage(0, 0)
    hide_stage(1, 0)
    for stage in range(1, final_stage):
        token_stage(1, stage)
        hidden_stage(0, stage)
        hide_stage(1, stage)
    hidden_stage(0, final_stage)
    project(0)
    token_stage(1, final_stage)
    hide_stage(1, final_stage)
    hidden_copy_own(1).start()
    hidden_stage(1, 0)
    hidden_stage(1, 1)
    give_back(0)
    for stage in range(2, final_stage + 1):
        hidden_stage(1, stage)
    project(1)
    give_back(1)
    combine(0)
    combine(1)

    for g in range(2):
        for c in range(CHUNKS):
            wait(slabs.at[g, c, : slots - SLAB], slab_send.at[g, c])
            for direction in range(2):
                for hop in range(hops(direction, c)):
                    wait(tokens.at[g, c, 0], token_send.at[g, direction, c, hop])
        for half in range(2):
            for direction in range(2):
                for hop in range(hops(direction, half)):
                    wait(hidden_part(g, half, 0), hidden_send.at[g, direction, half, hop])
        wait(columns.at[g, : ring - 1], columns_send.at[g])
        wait(spread.at[g, :, : slots - SLAB], final_send.at[g])

        @pl.when(jnp.logical_not(last(g)))
        def _(g=g):
            wait(spread.at[g, :, :SLAB], final_send_same.at[g])
            wait(residual.at[g], residual_send.at[g])
            wait(mixing.at[g], mixing_send.at[g])


def body(
    sections,
    act_down,
    act_up,
    norm_gain,
    gate_weight,
    up_weight,
    down_weight,
    routes_down,
    gates_down,
    routes_up,
    gates_up,
):
    count, depth = act_down.shape[1:]
    units = gate_weight.shape[1]
    hidden_units, piece = down_weight.shape[1:]
    ring = depth // piece
    rows, slots, width = EXPERTS * CAP, EXPERTS * SLAB, depth // CHUNKS
    half = -(-ring // 2)
    route_rows = jnp.concatenate([routes_down[0].T, routes_up[0].T], axis=0)
    dma = pltpu.SemaphoreType.DMA
    vmem = pl.BlockSpec(memory_space=pltpu.VMEM)
    outs = pl.pallas_call(
        functools.partial(kernel, EXPERTS, sections),
        out_shape=[jax.ShapeDtypeStruct((count, depth), BF16)] * 2,
        in_specs=[vmem] * 11,
        out_specs=[vmem] * 2,
        scratch_shapes=[
            pltpu.VMEM((2 * units, depth), BF16),
            pltpu.VMEM((2, count, depth), BF16),
            pltpu.VMEM((2, CHUNKS, slots, width), BF16),
            pltpu.VMEM((2, CHUNKS, slots, width), BF16),
            pltpu.VMEM((2, CHUNKS, ring, rows, width), BF16),
            pltpu.VMEM((2, ring * rows, units), BF16),
            pltpu.VMEM((2, ring * rows, hidden_units), BF16),
            pltpu.VMEM((2, ring, rows, piece), BF16),
            pltpu.VMEM((2, ring, rows, piece), BF16),
            pltpu.VMEM((2, ring // 2, slots, 2 * piece), BF16),
            pltpu.VMEM((2, ring // 2, slots, 2 * piece), BF16),
            pltpu.VMEM((2, count, depth), BF16),
            pltpu.VMEM((2, count, slots), F32),
            pltpu.VMEM((2, count, slots), F32),
            dma((2, CHUNKS)),
            dma((2, CHUNKS)),
            dma((2, 2, CHUNKS, half)),
            dma((2, 2, CHUNKS, half)),
            dma((2, 2, 2, half)),
            dma((2, 2, 2, half)),
            dma((2,)),
            dma((2,)),
            dma((2,)),
            dma((2,)),
            dma((2,)),
            dma((2,)),
            dma((2,)),
            dma((2,)),
            dma((2,)),
            dma((2,)),
        ],
        compiler_params=pltpu.CompilerParams(
            collective_id=0, has_side_effects=True, vmem_limit_bytes=56 * 1024 * 1024
        ),
    )(
        act_down[0],
        act_up[0],
        norm_gain,
        gate_weight[0],
        up_weight[0],
        down_weight[0],
        route_rows,
        routes_down[0],
        routes_up[0],
        gates_down[0],
        gates_up[0],
    )
    return tuple(out[None] for out in outs)


def solution(mesh):
    return jax.shard_map(
        functools.partial(body, mesh.shape["pipe"]),
        mesh=mesh,
        in_specs=(
            P("pipe", "expert", None),
            P("pipe", "expert", None),
            P("pipe", None),
            P("pipe", "expert", None),
            P("pipe", "expert", None),
            P("pipe", None, "expert"),
            P("pipe", "expert", None),
            P("pipe", "expert", None),
            P("pipe", "expert", None),
            P("pipe", "expert", None),
        ),
        out_specs=(P("pipe", "expert", None), P("pipe", "expert", None)),
        check_vma=False,
    )
```

time: 770 us -> 215 us (0.28)
  waiting for transfers between devices: 503 us -> 0 us
  starting transfers between devices: 207 us -> 0 us
  Pallas kernels: 0 us -> 204 us
  local copies, waits for them, and re-layouts: 32.9 us -> 8.41 us
  matrix products: 17.9 us -> 0 us
    all_to_all x4 -> x0, waiting for transfers between devices: 430 us -> none  [the longest x2 411 us: apply_layer(): lax.all_to_all(buffer, 'expert', split_axis=0, concat_axis=0, tiled=True)]
    pallas_call x0 -> x1, Pallas kernels: none -> 204 us  [body(): pl.pallas_call(functools.partial(kernel, EXPERTS, sections), out_shape=[j...]
    all_to_all x4 -> x0, starting transfers between devices: 131 us -> none  [the longest x2 74.8 us: expert_rows(): lax.all_to_all(shaped, 'expert', split_axis=0, concat_axis=0, tiled=True)]
    ppermute x8 -> x0, starting transfers between devices: 76.6 us -> none  [the longest x6 38.3 us: swapped(): return lax.ppermute(value, axis, pairs)]
    ppermute x8 -> x0, waiting for transfers between devices: 72.7 us -> none  [the longest x6 68.1 us: swapped(): return lax.ppermute(value, axis, pairs)]
    reshape x8 -> x0, local copies, waits for them, and re-layouts: 24.7 us -> none  [the longest x2 16 us: expert_rows(): flattened = received.reshape(-1, received.shape[-1])]
    dot_general x10 -> x0, matrix products: 17.9 us -> none  [the longest x2 7.77 us: expert_rows(): lax.dot_general(flattened, gate_rows, dims, preferred_element_type=jnp.fl...]
  transfers between devices with their start and end apart: 12 -> 0, of which waited for: 7 -> 0; matrix products, arithmetic and copies ran while one was open for 6% -> 0% of each run, Pallas kernels for 0% -> 0%
where the time goes in v1:
time: 215 us; the launch traced here: 214 us
  Pallas kernels  204 us (95%)
  local copies, waits for them, and re-layouts  8.41 us (4%)
    pallas_call x1, Pallas kernels, body(): pl.pallas_call(functools.partial(kernel, EXPERTS, sections), out_shape=[j...  204 us
    unnamed x13, local copies, waits for them, and re-layouts  5.59 us

profile of v1, /device:TPU:1, one launch (start us, length us, event | category | flops | bytes accessed | tf_op | source)
XLA Modules:
  0.0 213.6 jit_solution(12120683222622237345)
XLA Ops:
  0.6 0.0 copy-start.1
  0.6 0.0 copy-start.2
  0.7 0.6 copy-done.1
  1.3 0.0 copy-done.2
  1.3 0.0 copy-start.3
  1.3 0.6 pad_add_fusion.route_rows
  1.9 0.1 copy-done.3
  2.0 0.0 copy-start.4
  2.0 0.7 copy.15.gate_cols_down
  2.7 0.0 copy-done.4
  2.7 0.7 copy.16.gate_cols_up
  3.4 0.7 copy.14.route_cols_up
  4.1 0.7 copy.13.route_cols_down
  4.8 2.2 %copy.12 = bf16[1,1024,448]{2,1,0:T(8,128)(2,1)} copy(bf16[1,1024,448]{1,2,0:T(8,128)(2,1)} %param.15) | data formatting | bytes 1835008 | tf_op args[5]
  7.0 204.0 %shard_map.113 = (bf16[64,3584]{1,0:T(8,128)(2,1)}, bf16[64,3584]{1,0:T(8,128)(2,1)}) custom-call(bf16[64,3584]{1,0:T(8,128)(2,1)} %bitcast.16, bf16[64,3584]{1,0:T(8,128)(2,1)} %bitcast.17, bf16[1,3584]{1,0:T(2,128)(2,1)} %gain.1, bf16[128,3584]{1,0:T(8,128)(2,1)} %bitcast.14, bf16[128,3584]{1,0:T(8,128)(2,1)} %bitcast.15, bf16[1024,448]{1,0:T(8,128)(2,1)} %bitcast.13, ...), custom_call_target="tpu_custom_call" | custom-call | tf_op jit(solution)/shard_map/pallas_call | solution.py:494
  211.0 0.0 copy-start
  211.0 1.9 copy.19
  212.9 0.0 copy-done
  212.9 0.8 copy.20
Async XLA Ops:
  0.6 0.7 copy-start.1
  0.6 0.7 copy-start.2
  1.3 0.7 copy-start.3
  2.0 0.7 copy-start.4
  211.0 1.9 copy-start

commit v2 on v0

v2 whole, which is shorter than its diff:
```python
import functools

import jax
import jax.numpy as jnp
from jax import lax
from jax.experimental import pallas as pl
from jax.experimental.pallas import tpu as pltpu
from jax.sharding import PartitionSpec as P

EXPERTS = 8
CAP = 10
SLAB = 16
FOLD = 4
OFFSET = 1
EPSILON = 1e-06

MESH = pl.DeviceIdType.MESH
F32 = jnp.float32
BF16 = jnp.bfloat16


def one_hot(condition):
    return jnp.where(condition, 1.0, 0.0).astype(BF16)


def iota(shape, dimension):
    return lax.broadcasted_iota(jnp.int32, shape, dimension)


def dot_t(a, b):
    return lax.dot_general(a, b, (((1,), (1,)), ((), ())), preferred_element_type=F32)


def kernel(
    experts,
    sections,
    x_down,
    x_up,
    gain,
    routes_down,
    routes_up,
    gates_down,
    gates_up,
    gate_w,
    up_w,
    down_w,
    out_down,
    out_up,
    gate_up,
    down,
    normed,
    slabs,
    landed,
    tokens,
    hidden_own,
    hidden,
    columns,
    returned,
    spread,
    final,
    residual,
    notes,
    notes_here,
    weight_copy,
    slab_send,
    slab_recv,
    token_send,
    token_recv,
    hidden_send,
    hidden_recv,
    hidden_copy,
    columns_send,
    columns_recv,
    final_send,
    final_send_same,
    final_recv,
    residual_send,
    residual_recv,
    notes_send,
    notes_recv,
):
    groups, ring = tokens.shape[:2]
    per = SLAB // FOLD
    rows = experts * per
    slots = experts * SLAB
    count, depth = x_down.shape
    width = depth // FOLD
    units = gate_w.shape[0]
    pipe = lax.axis_index("pipe")
    position = lax.axis_index("expert")
    y = position // ring
    z = position % ring
    x_refs = (x_down, x_up)
    routes = (routes_down, routes_up)
    gates = (gates_down, gates_up)
    outs = (out_down, out_up)

    def groups_of(stream):
        return range(stream * CAP // per, -(-(stream + 1) * CAP // per))

    def streams_of(g):
        return [stream for stream in range(2) if g in groups_of(stream)]

    def at_y(k):
        return (pipe, lax.rem(y + k, experts) * ring + z)

    def at_z(k):
        return (pipe, y * ring + lax.rem(z + k, ring))

    barrier = pltpu.get_barrier_semaphore()

    def greet(device):
        pl.semaphore_signal(barrier, inc=1, device_id=device, device_id_type=MESH)

    @pl.loop(1, experts)
    def _(k):
        greet(at_y(k))

    @pl.loop(1, ring)
    def _(k):
        greet(at_z(k))

    @pl.when(pipe > 0)
    def _():
        @pl.loop(0, experts)
        def _(k):
            greet((pipe - 1, k * ring + z))

    @pl.when(pipe < sections - 1)
    def _():
        @pl.loop(0, experts)
        def _(k):
            greet((pipe + 1, k * ring + z))

    neighbours = jnp.where(pipe > 0, 1, 0) + jnp.where(pipe < sections - 1, 1, 0)
    greeted = experts - 1 + ring - 1 + experts * neighbours

    weight_copies = (
        pltpu.make_async_copy(gate_w, gate_up.at[:units], weight_copy.at[0]),
        pltpu.make_async_copy(up_w, gate_up.at[units:], weight_copy.at[1]),
        pltpu.make_async_copy(down_w, down, weight_copy.at[2]),
    )
    for copy in weight_copies:
        copy.start()

    def wait(ref, sem):
        pltpu.make_async_copy(ref, ref, sem).wait()

    def remote(source, target, sent, received, device):
        return pltpu.make_async_remote_copy(
            src_ref=source,
            dst_ref=target,
            send_sem=sent,
            recv_sem=received,
            device_id=device,
            device_id_type=MESH,
        )

    def normalize(stream):
        x_ref = x_refs[stream]
        total = jnp.zeros((count, 1), F32)
        for c in range(FOLD):
            part = x_ref[:, c * width : (c + 1) * width].astype(F32)
            total = total + jnp.sum(part * part, axis=-1, keepdims=True)
        inverse = lax.rsqrt(total / depth + EPSILON)
        for c in range(FOLD):
            cut = slice(c * width, (c + 1) * width)
            part = x_ref[:, cut].astype(F32)
            normed[stream, :, cut] = (part * inverse * gain[:, cut].astype(F32)).astype(BF16)

    def number(stream):
        named = one_hot(routes[stream][...] == iota((experts, count), 0))
        earlier = one_hot(iota((count, count), 0) < iota((count, count), 1))
        rank = jnp.dot(named, earlier, preferred_element_type=F32)
        slot = jnp.sum(named.astype(F32) * rank, axis=0, keepdims=True) + stream * CAP
        expert = routes[stream][...].astype(F32)
        row = iota((128, count), 0)
        table = jnp.where(row == 0, expert, jnp.where(row == 1, slot, gates[stream][...]))
        notes[stream] = jnp.transpose(table)
        return expert, slot

    def slab(k):
        return pl.ds(pl.multiple_of(k * SLAB, SLAB), SLAB)

    def matches(g, place, expert, slot):
        inside = place % per + g * per
        return (expert == (place // SLAB).astype(F32)) & (slot == inside.astype(F32))

    def dispatch(g, numbers):
        place = iota((slots, count), 0)
        total = jnp.zeros((slots, width), F32)
        for stream in streams_of(g):
            chosen = matches(g, place, *numbers[stream])
            for c in range(FOLD):
                total = total + jnp.dot(
                    one_hot(chosen & (place // per % FOLD == c)),
                    normed[stream, :, c * width : (c + 1) * width],
                    preferred_element_type=F32,
                )
        slabs[g] = total.astype(BF16)
        pltpu.make_async_copy(
            slabs.at[g, slab(y)], landed.at[g, slab(y)], slab_recv.at[g]
        ).start()

        @pl.loop(1, experts)
        def _(k):
            remote(
                slabs.at[g, slab(lax.rem(y + k, experts))],
                landed.at[g, slab(y)],
                slab_send.at[g],
                slab_recv.at[g],
                at_y(k),
            ).start()

    def last(stream):
        return pipe == (sections - 1 if stream == 0 else 0)

    def onward(stream):
        return pipe + 1 if stream == 0 else pipe - 1

    def send_residual(stream):
        pairs = (
            (x_refs[stream], residual, residual_send, residual_recv),
            (notes.at[stream], notes_here, notes_send, notes_recv),
        )

        @pl.when(last(stream))
        def _():
            for source, target, _, sem in pairs:
                end = 1 - stream
                pltpu.make_async_copy(source, target.at[end], sem.at[end]).start()

        @pl.when(jnp.logical_not(last(stream)))
        def _():
            for source, target, sent, sem in pairs:
                remote(
                    source,
                    target.at[stream],
                    sent.at[stream],
                    sem.at[stream],
                    (onward(stream), position),
                ).start()

    def hops(direction, part):
        return ring // 2 if direction == part % 2 else ring - 1 - ring // 2

    def behind(direction, k):
        return lax.rem(z + (ring - k if direction == 0 else k), ring)

    def ahead(direction):
        return at_z(1 if direction == 0 else ring - 1)

    half = FOLD * rows // 2

    def token_part(g, part, owner):
        return tokens.at[g, owner, part * half : (part + 1) * half]

    def token_ring(g, part, direction, hop):
        block = token_part(g, part, behind(direction, hop))
        return remote(
            block,
            block,
            token_send.at[g, part, direction, hop],
            token_recv.at[g, part, direction, hop],
            ahead(direction),
        )

    def token_stage(g, stage):
        for part in range(2):
            for direction in range(2):
                if 1 <= stage <= hops(direction, part):
                    wait(
                        token_part(g, part, behind(direction, stage)),
                        token_recv.at[g, part, direction, stage - 1],
                    )
                if stage < hops(direction, part):
                    token_ring(g, part, direction, stage).start()

    def compact(g):
        wait(landed.at[g], slab_recv.at[g])
        size = FOLD * rows
        row, place = iota((size, slots), 0), iota((size, slots), 1)
        same = row // rows == place // per % FOLD
        same = same & (row % rows == place // SLAB * per + place % per)
        tokens[g, z] = jnp.dot(
            one_hot(same), landed[g], preferred_element_type=F32
        ).astype(BF16)

    def hide(g):
        total = jnp.zeros((ring * rows, 2 * units), F32)
        for c in range(FOLD):
            part = tokens[g, :, c * rows : (c + 1) * rows, :].reshape(ring * rows, width)
            total = total + dot_t(part, gate_up[:, c * width : (c + 1) * width])
        hidden_own[g] = (jax.nn.silu(total[:, :units]) * total[:, units:]).astype(BF16)

    def hidden_part(g, owner):
        return hidden.at[g, :, pl.ds(pl.multiple_of(owner * units, units), units)]

    def hidden_copy_own(g):
        return pltpu.make_async_copy(hidden_own.at[g], hidden_part(g, z), hidden_copy.at[g])

    def hidden_stage(g, stage):
        if stage == 0:
            hidden_copy_own(g).start()
        for direction in range(2):
            if 1 <= stage <= hops(direction, g):
                wait(
                    hidden_part(g, behind(direction, stage)),
                    hidden_recv.at[g, direction, stage - 1],
                )
            if stage < hops(direction, g):
                block = hidden_part(g, behind(direction, stage))
                remote(
                    hidden_own.at[g] if stage == 0 else block,
                    block,
                    hidden_send.at[g, direction, stage],
                    hidden_recv.at[g, direction, stage],
                    ahead(direction),
                ).start()

    def project(g):
        hidden_copy_own(g).wait()
        result = dot_t(hidden[g], down[...]).astype(BF16)
        piece = rows // 2
        for b in range(ring):
            first, second = (
                result[(2 * b + i) * piece : (2 * b + i + 1) * piece] for i in range(2)
            )
            columns[g, b] = jnp.concatenate([first, second], axis=1)
        target = returned.at[g, z % 2, z // 2]
        pltpu.make_async_copy(columns.at[g, z], target, columns_recv.at[g]).start()

        @pl.loop(1, ring)
        def _(k):
            remote(
                columns.at[g, lax.rem(z + k, ring)],
                target,
                columns_send.at[g],
                columns_recv.at[g],
                at_z(k),
            ).start()

    def give_back(g):
        wait(returned.at[g], columns_recv.at[g])
        size, piece = slots // 2, rows // 2
        row, place = iota((size, size), 0), iota((size, size), 1)
        same = row // per % FOLD == place // piece
        same = same & (row // SLAB * per + row % per == place % piece)
        order = one_hot(same)
        even, odd = (
            jnp.dot(
                order,
                returned[g, i].reshape(size, width),
                preferred_element_type=F32,
            )
            for i in range(2)
        )
        cut = width // 2
        for i in range(2):
            lanes = slice(i * cut, (i + 1) * cut)
            joined = jnp.concatenate([even[:, lanes], odd[:, lanes]], axis=1)
            spread[g, i * size : (i + 1) * size] = joined.astype(BF16)
        for stream in streams_of(g):
            send_back(g, stream)

    def send_back(g, stream):
        index = g - groups_of(stream)[0]

        @pl.when(last(stream))
        def _():
            end = 1 - stream
            target = final.at[end, index, slab(y)]
            pltpu.make_async_copy(
                spread.at[g, slab(y)], target, final_recv.at[end, index]
            ).start()

            @pl.loop(1, experts)
            def _(k):
                remote(
                    spread.at[g, slab(lax.rem(y + k, experts))],
                    target,
                    final_send.at[stream, index],
                    final_recv.at[end, index],
                    at_y(k),
                ).start()

        @pl.when(jnp.logical_not(last(stream)))
        def _():
            target = final.at[stream, index, slab(y)]
            remote(
                spread.at[g, slab(y)],
                target,
                final_send_same.at[stream, index],
                final_recv.at[stream, index],
                (onward(stream), position),
            ).start()

            @pl.loop(1, experts)
            def _(k):
                to = lax.rem(y + k, experts)
                remote(
                    spread.at[g, slab(to)],
                    target,
                    final_send.at[stream, index],
                    final_recv.at[stream, index],
                    (onward(stream), to * ring + z),
                ).start()

    def combine(end):
        wait(residual.at[end], residual_recv.at[end])
        wait(notes_here.at[end], notes_recv.at[end])
        place = iota((count, slots), 1)
        note = notes_here[end]
        expert, slot, weight = note[:, 0:1], note[:, 1:2], note[:, 2:3]
        turned = jnp.where(pipe == 0, end == 0, (pipe == sections - 1) & (end == 1))
        stream = jnp.where(turned, 1 - end, end)
        start = stream * CAP // per * per
        chosen = []
        for index in range(len(groups_of(0))):
            wait(final.at[end, index], final_recv.at[end, index])
            inside = place % per + index * per + start
            chosen.append(
                (expert == (place // SLAB).astype(F32)) & (slot == inside.astype(F32))
            )
        for c in range(FOLD):
            cut = slice(c * width, (c + 1) * width)
            picked = jnp.zeros((count, width), F32)
            for index, choice in enumerate(chosen):
                picked = picked + jnp.dot(
                    one_hot(choice & (place // per % FOLD == c)),
                    final[end, index],
                    preferred_element_type=F32,
                )
            outs[end][:, cut] = (residual[end, :, cut].astype(F32) + weight * picked).astype(BF16)

    numbers = [None, None]
    for stream in range(2):
        normalize(stream)
        numbers[stream] = number(stream)
        if stream == 0:
            pl.semaphore_wait(barrier, greeted)
        for g in range(groups):
            if streams_of(g)[-1] == stream:
                dispatch(g, numbers)
        send_residual(stream)
    for copy in weight_copies:
        copy.wait()

    stages = ring // 2

    def action(g, step):
        if step == 0:
            compact(g)
        if step <= stages:
            token_stage(g, step)
        if step == stages:
            hide(g)
        if stages <= step <= 2 * stages:
            hidden_stage(g, step - stages)
        if step == 2 * stages:
            project(g)
        if step == 2 * stages + 1:
            give_back(g)

    final_step = 2 * stages + 1
    for step in range((groups - 1) * OFFSET + final_step + 1):
        for g in range(groups):
            if 0 <= step - g * OFFSET <= final_step:
                action(g, step - g * OFFSET)
    combine(0)
    combine(1)

    for g in range(groups):
        wait(slabs.at[g, : slots - SLAB], slab_send.at[g])
        for direction in range(2):
            for part in range(2):
                for hop in range(hops(direction, part)):
                    wait(token_part(g, part, 0), token_send.at[g, part, direction, hop])
            for hop in range(hops(direction, g)):
                wait(hidden_own.at[g], hidden_send.at[g, direction, hop])
        wait(columns.at[g, : ring - 1], columns_send.at[g])
    for stream in range(2):
        for index in range(len(groups_of(stream))):
            wait(spread.at[0, : slots - SLAB], final_send.at[stream, index])

        @pl.when(jnp.logical_not(last(stream)))
        def _(stream=stream):
            for index in range(len(groups_of(stream))):
                wait(spread.at[0, :SLAB], final_send_same.at[stream, index])
            wait(residual.at[stream], residual_send.at[stream])
            wait(notes.at[stream], notes_send.at[stream])


def body(
    sections,
    act_down,
    act_up,
    norm_gain,
    gate_weight,
    up_weight,
    down_weight,
    routes_down,
    gates_down,
    routes_up,
    gates_up,
):
    count, depth = act_down.shape[1:]
    units = gate_weight.shape[1]
    hidden_units, piece = down_weight.shape[1:]
    ring = depth // piece
    per = SLAB // FOLD
    groups = 2 * CAP // per
    mine = -(-CAP // per)
    rows, slots, width = EXPERTS * per, EXPERTS * SLAB, depth // FOLD
    half = ring // 2
    dma = pltpu.SemaphoreType.DMA
    vmem = pl.BlockSpec(memory_space=pltpu.VMEM)
    anywhere = pl.BlockSpec(memory_space=pl.ANY)
    outs = pl.pallas_call(
        functools.partial(kernel, EXPERTS, sections),
        out_shape=[jax.ShapeDtypeStruct((count, depth), BF16)] * 2,
        in_specs=[vmem] * 7 + [anywhere] * 3,
        out_specs=[vmem] * 2,
        scratch_shapes=[
            pltpu.VMEM((2 * units, depth), BF16),
            pltpu.VMEM((piece, hidden_units), BF16),
            pltpu.VMEM((2, count, depth), BF16),
            pltpu.VMEM((groups, slots, width), BF16),
            pltpu.VMEM((groups, slots, width), BF16),
            pltpu.VMEM((groups, ring, FOLD * rows, width), BF16),
            pltpu.VMEM((groups, ring * rows, units), BF16),
            pltpu.VMEM((groups, ring * rows, hidden_units), BF16),
            pltpu.VMEM((groups, ring, rows // 2, 2 * piece), BF16),
            pltpu.VMEM((groups, 2, ring // 2, rows // 2, 2 * piece), BF16),
            pltpu.VMEM((groups, slots, width), BF16),
            pltpu.VMEM((2, mine, slots, width), BF16),
            pltpu.VMEM((2, count, depth), BF16),
            pltpu.VMEM((2, count, 128), F32),
            pltpu.VMEM((2, count, 128), F32),
            dma((3,)),
            dma((groups,)),
            dma((groups,)),
            dma((groups, 2, 2, half)),
            dma((groups, 2, 2, half)),
            dma((groups, 2, half)),
            dma((groups, 2, half)),
            dma((groups,)),
            dma((groups,)),
            dma((groups,)),
            dma((2, mine)),
            dma((2, mine)),
            dma((2, mine)),
            dma((2,)),
            dma((2,)),
            dma((2,)),
            dma((2,)),
        ],
        compiler_params=pltpu.CompilerParams(
            collective_id=0, has_side_effects=True, vmem_limit_bytes=56 * 1024 * 1024
        ),
    )(
        act_down[0],
        act_up[0],
        norm_gain,
        routes_down[0].T,
        routes_up[0].T,
        gates_down[0].T,
        gates_up[0].T,
        gate_weight[0],
        up_weight[0],
        down_weight[0].T,
    )
    return tuple(out[None] for out in outs)


def solution(mesh):
    return jax.shard_map(
        functools.partial(body, mesh.shape["pipe"]),
        mesh=mesh,
        in_specs=(
            P("pipe", "expert", None),
            P("pipe", "expert", None),
            P("pipe", None),
            P("pipe", "expert", None),
            P("pipe", "expert", None),
            P("pipe", None, "expert"),
            P("pipe", "expert", None),
            P("pipe", "expert", None),
            P("pipe", "expert", None),
            P("pipe", "expert", None),
        ),
        out_specs=(P("pipe", "expert", None), P("pipe", "expert", None)),
        check_vma=False,
    )
```

time: 770 us -> 185 us (0.24)
  waiting for transfers between devices: 503 us -> 0 us
  starting transfers between devices: 207 us -> 0 us
  Pallas kernels: 0 us -> 182 us
  local copies, waits for them, and re-layouts: 32.9 us -> 2.64 us
  matrix products: 17.9 us -> 0 us
    all_to_all x4 -> x0, waiting for transfers between devices: 430 us -> none  [the longest x2 411 us: apply_layer(): lax.all_to_all(buffer, 'expert', split_axis=0, concat_axis=0, tiled=True)]
    pallas_call x0 -> x1, Pallas kernels: none -> 182 us  [body(): pl.pallas_call(functools.partial(kernel, EXPERTS, sections), out_shape=[j...]
    all_to_all x4 -> x0, starting transfers between devices: 131 us -> none  [the longest x2 74.8 us: expert_rows(): lax.all_to_all(shaped, 'expert', split_axis=0, concat_axis=0, tiled=True)]
    ppermute x8 -> x0, starting transfers between devices: 76.6 us -> none  [the longest x6 38.3 us: swapped(): return lax.ppermute(value, axis, pairs)]
    ppermute x8 -> x0, waiting for transfers between devices: 72.7 us -> none  [the longest x6 68.1 us: swapped(): return lax.ppermute(value, axis, pairs)]
    reshape x8 -> x0, local copies, waits for them, and re-layouts: 24.7 us -> none  [the longest x2 16 us: expert_rows(): flattened = received.reshape(-1, received.shape[-1])]
    dot_general x10 -> x0, matrix products: 17.9 us -> none  [the longest x2 7.77 us: expert_rows(): lax.dot_general(flattened, gate_rows, dims, preferred_element_type=jnp.fl...]
  transfers between devices with their start and end apart: 12 -> 0, of which waited for: 7 -> 0; matrix products, arithmetic and copies ran while one was open for 6% -> 0% of each run, Pallas kernels for 0% -> 0%
where the time goes in v2:
time: 185 us
  Pallas kernels  182 us (98%)
  local copies, waits for them, and re-layouts  2.64 us (1%)
    pallas_call x1, Pallas kernels, body(): pl.pallas_call(functools.partial(kernel, EXPERTS, sections), out_shape=[j...  182 us

profile of v2, /device:TPU:1, one launch (start us, length us, event | category | flops | bytes accessed | tf_op | source)
XLA Modules:
  0.0 184.8 jit_solution(18430528896578360284)
XLA Ops:
  0.6 181.5 %shard_map.113 = (bf16[64,3584]{1,0:T(8,128)(2,1)}, bf16[64,3584]{1,0:T(8,128)(2,1)}) custom-call(bf16[64,3584]{1,0:T(8,128)(2,1)} %bitcast.16, bf16[64,3584]{1,0:T(8,128)(2,1)} %bitcast.17, bf16[1,3584]{1,0:T(2,128)(2,1)} %gain.1, s32[1,64]{1,0:T(1,128)} %bitcast.20, s32[1,64]{1,0:T(1,128)} %bitcast.21, f32[1,64]{1,0:T(1,128)} %bitcast.22, ...), custom_call_target="tpu_custom_call" | custom-call | tf_op jit(solution)/shard_map/pallas_call | solution.py:519
  182.2 0.0 copy-start
  182.2 1.9 %copy.14 = bf16[1,64,3584]{2,1,0:T(8,128)(2,1)} copy(bf16[1,64,3584]{2,1,0:T(8,128)(2,1)} %bitcast.19) | data formatting | bytes 917504
  184.0 0.0 copy-done
  184.0 0.8 copy.15
Async XLA Ops:
  182.2 1.9 %copy-start = (bf16[64,3584]{1,0:T(8,128)(2,1)S(1)}, bf16[64,3584]{1,0:T(8,128)(2,1)}, u32[]{:S(2)}) copy-start(bf16[64,3584]{1,0:T(8,128)(2,1)} %get-tuple-element.5) | copy-start | bytes 1376260

commit v3 on v2

--- a/solution.py
+++ b/solution.py
@@ -49,6 +49,11 @@
     gate_up,
     down,
     normed,
+    raw,
+    table,
+    tables,
+    slabs_raw,
+    landed_raw,
     slabs,
     landed,
     tokens,
@@ -61,7 +66,14 @@
     residual,
     notes,
     notes_here,
+    sums,
     weight_copy,
+    raw_send,
+    raw_recv,
+    table_send,
+    table_recv,
+    slab_raw_send,
+    slab_raw_recv,
     slab_send,
     slab_recv,
     token_send,
@@ -166,7 +178,11 @@
         for c in range(FOLD):
             cut = slice(c * width, (c + 1) * width)
             part = x_ref[:, cut].astype(F32)
-            normed[stream, :, cut] = (part * inverse * gain[:, cut].astype(F32)).astype(BF16)
+            scaled = (part * inverse * gain[:, cut].astype(F32)).astype(BF16)
+            if c == 0:
+                raw[z, stream * count : (stream + 1) * count] = scaled
+            else:
+                normed[stream, :, cut] = scaled
 
     def number(stream):
         named = one_hot(routes[stream][...] == iota((experts, count), 0))
@@ -175,9 +191,20 @@
         slot = jnp.sum(named.astype(F32) * rank, axis=0, keepdims=True) + stream * CAP
         expert = routes[stream][...].astype(F32)
         row = iota((128, count), 0)
-        table = jnp.where(row == 0, expert, jnp.where(row == 1, slot, gates[stream][...]))
-        notes[stream] = jnp.transpose(table)
+        note = jnp.where(row == 0, expert, jnp.where(row == 1, slot, gates[stream][...]))
+        notes[stream] = jnp.transpose(note)
         return expert, slot
+
+    def send_table(numbers):
+        row = iota((8, 2 * count), 0)
+        expert, slot = (jnp.concatenate(pair, axis=1) for pair in zip(*numbers))
+        table[...] = jnp.where(row == 0, expert, slot)
+        target = tables.at[:, pl.ds(pl.multiple_of(z * 2 * count, 2 * count), 2 * count)]
+        pltpu.make_async_copy(table, target, table_recv).start()
+
+        @pl.loop(1, ring)
+        def _(k):
+            remote(table, target, table_send, table_recv, at_z(k)).start()
 
     def slab(k):
         return pl.ds(pl.multiple_of(k * SLAB, SLAB), SLAB)
@@ -186,18 +213,20 @@
         inside = place % per + g * per
         return (expert == (place // SLAB).astype(F32)) & (slot == inside.astype(F32))
 
-    def dispatch(g, numbers):
+    def pack(g, numbers):
         place = iota((slots, count), 0)
         total = jnp.zeros((slots, width), F32)
         for stream in streams_of(g):
             chosen = matches(g, place, *numbers[stream])
-            for c in range(FOLD):
+            for c in range(1, FOLD):
                 total = total + jnp.dot(
                     one_hot(chosen & (place // per % FOLD == c)),
                     normed[stream, :, c * width : (c + 1) * width],
                     preferred_element_type=F32,
                 )
         slabs[g] = total.astype(BF16)
+
+    def dispatch(g):
         pltpu.make_async_copy(
             slabs.at[g, slab(y)], landed.at[g, slab(y)], slab_recv.at[g]
         ).start()
@@ -250,7 +279,57 @@
     def ahead(direction):
         return at_z(1 if direction == 0 else ring - 1)
 
-    half = FOLD * rows // 2
+    half = (FOLD - 1) * rows // 2
+
+    def raw_ring(part, direction, hop):
+        block = raw.at[behind(direction, hop), part * count : (part + 1) * count]
+        return remote(
+            block,
+            block,
+            raw_send.at[part, direction, hop],
+            raw_recv.at[part, direction, hop],
+            ahead(direction),
+        )
+
+    def raw_stage(part, stage):
+        for direction in range(2):
+            if 1 <= stage <= hops(direction, part):
+                wait(
+                    raw.at[behind(direction, stage), part * count : (part + 1) * count],
+                    raw_recv.at[part, direction, stage - 1],
+                )
+            if stage < hops(direction, part):
+                raw_ring(part, direction, stage).start()
+
+    def dispatch_raw(g):
+        if g == 0:
+            wait(tables, table_recv)
+        size, span = ring * rows, ring * 2 * count
+        row, lane = iota((size, span), 0), iota((size, span), 1)
+        inside = row % per + g * per
+        chosen = tables[0:1, :] == (row // (ring * per)).astype(F32)
+        chosen = chosen & (tables[1:2, :] == inside.astype(F32))
+        chosen = chosen & (row // per % ring == lane // (2 * count))
+        slabs_raw[g] = jnp.dot(
+            one_hot(chosen), raw[...].reshape(span, width), preferred_element_type=F32
+        ).astype(BF16)
+
+        def part(k):
+            return pl.ds(pl.multiple_of(k * ring * per, ring * per), ring * per)
+
+        pltpu.make_async_copy(
+            slabs_raw.at[g, part(y)], landed_raw.at[g, part(y)], slab_raw_recv.at[g]
+        ).start()
+
+        @pl.loop(1, experts)
+        def _(k):
+            remote(
+                slabs_raw.at[g, part(lax.rem(y + k, experts))],
+                landed_raw.at[g, part(y)],
+                slab_raw_send.at[g],
+                slab_raw_recv.at[g],
+                at_y(k),
+            ).start()
 
     def token_part(g, part, owner):
         return tokens.at[g, owner, part * half : (part + 1) * half]
@@ -278,18 +357,24 @@
 
     def compact(g):
         wait(landed.at[g], slab_recv.at[g])
-        size = FOLD * rows
+        size = (FOLD - 1) * rows
         row, place = iota((size, slots), 0), iota((size, slots), 1)
-        same = row // rows == place // per % FOLD
+        same = row // rows + 1 == place // per % FOLD
         same = same & (row % rows == place // SLAB * per + place % per)
         tokens[g, z] = jnp.dot(
             one_hot(same), landed[g], preferred_element_type=F32
         ).astype(BF16)
 
     def hide(g):
-        total = jnp.zeros((ring * rows, 2 * units), F32)
-        for c in range(FOLD):
-            part = tokens[g, :, c * rows : (c + 1) * rows, :].reshape(ring * rows, width)
+        wait(landed_raw.at[g], slab_raw_recv.at[g])
+        size = ring * rows
+        row, place = iota((size, size), 0), iota((size, size), 1)
+        same = (row // rows == place // per % ring) & (row % per == place % per)
+        same = same & (row // per % experts == place // (ring * per))
+        part = jnp.dot(one_hot(same), landed_raw[g], preferred_element_type=F32)
+        total = dot_t(part.astype(BF16), gate_up[:, :width])
+        for c in range(1, FOLD):
+            part = tokens[g, :, (c - 1) * rows : c * rows, :].reshape(size, width)
             total = total + dot_t(part, gate_up[:, c * width : (c + 1) * width])
         hidden_own[g] = (jax.nn.silu(total[:, :units]) * total[:, units:]).astype(BF16)
 
@@ -406,47 +491,53 @@
                     (onward(stream), to * ring + z),
                 ).start()
 
-    def combine(end):
-        wait(residual.at[end], residual_recv.at[end])
-        wait(notes_here.at[end], notes_recv.at[end])
+    def combine(end, index):
+        if index == 0:
+            wait(residual.at[end], residual_recv.at[end])
+            wait(notes_here.at[end], notes_recv.at[end])
+        wait(final.at[end, index], final_recv.at[end, index])
         place = iota((count, slots), 1)
         note = notes_here[end]
         expert, slot, weight = note[:, 0:1], note[:, 1:2], note[:, 2:3]
         turned = jnp.where(pipe == 0, end == 0, (pipe == sections - 1) & (end == 1))
         stream = jnp.where(turned, 1 - end, end)
-        start = stream * CAP // per * per
-        chosen = []
-        for index in range(len(groups_of(0))):
-            wait(final.at[end, index], final_recv.at[end, index])
-            inside = place % per + index * per + start
-            chosen.append(
-                (expert == (place // SLAB).astype(F32)) & (slot == inside.astype(F32))
-            )
+        inside = place % per + index * per + stream * CAP // per * per
+        chosen = (expert == (place // SLAB).astype(F32)) & (slot == inside.astype(F32))
         for c in range(FOLD):
             cut = slice(c * width, (c + 1) * width)
-            picked = jnp.zeros((count, width), F32)
-            for index, choice in enumerate(chosen):
-                picked = picked + jnp.dot(
-                    one_hot(choice & (place // per % FOLD == c)),
-                    final[end, index],
-                    preferred_element_type=F32,
-                )
-            outs[end][:, cut] = (residual[end, :, cut].astype(F32) + weight * picked).astype(BF16)
-
-    numbers = [None, None]
+            picked = jnp.dot(
+                one_hot(chosen & (place // per % FOLD == c)),
+                final[end, index],
+                preferred_element_type=F32,
+            )
+            if index > 0:
+                picked = picked + sums[end, :, cut]
+            if index < len(groups_of(0)) - 1:
+                sums[end, :, cut] = picked
+            else:
+                total = residual[end, :, cut].astype(F32) + weight * picked
+                outs[end][:, cut] = total.astype(BF16)
+
+    normalize(0)
+    numbers = [number(0)]
+    pack(0, numbers)
+    pl.semaphore_wait(barrier, greeted)
+    raw_stage(0, 0)
+    dispatch(0)
+    normalize(1)
+    raw_stage(1, 0)
+    numbers.append(number(1))
+    send_table(numbers)
+    for g in range(1, groups):
+        pack(g, numbers)
+        dispatch(g)
     for stream in range(2):
-        normalize(stream)
-        numbers[stream] = number(stream)
-        if stream == 0:
-            pl.semaphore_wait(barrier, greeted)
-        for g in range(groups):
-            if streams_of(g)[-1] == stream:
-                dispatch(g, numbers)
         send_residual(stream)
     for copy in weight_copies:
         copy.wait()
 
     stages = ring // 2
+    final_step = 2 * stages + 1
 
     def action(g, step):
         if step == 0:
@@ -459,19 +550,30 @@
             hidden_stage(g, step - stages)
         if step == 2 * stages:
             project(g)
-        if step == 2 * stages + 1:
+        if step == final_step:
             give_back(g)
 
-    final_step = 2 * stages + 1
-    for step in range((groups - 1) * OFFSET + final_step + 1):
+    for step in range(1, (groups - 1) * OFFSET + final_step + 2):
+        if step <= stages:
+            for part in range(2):
+                raw_stage(part, step)
+        if 0 <= step - stages < groups:
+            dispatch_raw(step - stages)
         for g in range(groups):
-            if 0 <= step - g * OFFSET <= final_step:
-                action(g, step - g * OFFSET)
-    combine(0)
-    combine(1)
-
+            if 0 <= step - 1 - g * OFFSET <= final_step:
+                action(g, step - 1 - g * OFFSET)
+    for index in range(len(groups_of(0))):
+        for end in range(2):
+            combine(end, index)
+
+    wait(tables.at[:, : (ring - 1) * 2 * count], table_send)
+    for part in range(2):
+        for direction in range(2):
+            for hop in range(hops(direction, part)):
+                wait(raw.at[0, :count], raw_send.at[part, direction, hop])
     for g in range(groups):
         wait(slabs.at[g, : slots - SLAB], slab_send.at[g])
+        wait(slabs_raw.at[g, : (experts - 1) * ring * per], slab_raw_send.at[g])
         for direction in range(2):
             for part in range(2):
                 for hop in range(hops(direction, part)):
@@ -525,9 +627,14 @@
             pltpu.VMEM((2 * units, depth), BF16),
             pltpu.VMEM((piece, hidden_units), BF16),
             pltpu.VMEM((2, count, depth), BF16),
+            pltpu.VMEM((ring, 2 * count, width), BF16),
+            pltpu.VMEM((8, 2 * count), F32),
+            pltpu.VMEM((8, ring * 2 * count), F32),
+            pltpu.VMEM((groups, ring * rows, width), BF16),
+            pltpu.VMEM((groups, ring * rows, width), BF16),
             pltpu.VMEM((groups, slots, width), BF16),
             pltpu.VMEM((groups, slots, width), BF16),
-            pltpu.VMEM((groups, ring, FOLD * rows, width), BF16),
+            pltpu.VMEM((groups, ring, (FOLD - 1) * rows, width), BF16),
             pltpu.VMEM((groups, ring * rows, units), BF16),
             pltpu.VMEM((groups, ring * rows, hidden_units), BF16),
             pltpu.VMEM((groups, ring, rows // 2, 2 * piece), BF16),
@@ -537,7 +644,14 @@
             pltpu.VMEM((2, count, depth), BF16),
             pltpu.VMEM((2, count, 128), F32),
             pltpu.VMEM((2, count, 128), F32),
+            pltpu.VMEM((2, count, depth), F32),
             dma((3,)),
+            dma((2, 2, half)),
+            dma((2, 2, half)),
+            dma,
+            dma,
+            dma((groups,)),
+            dma((groups,)),
             dma((groups,)),
             dma((groups,)),
             dma((groups, 2, 2, half)),

time: 185 us -> 171 us (0.924)
  Pallas kernels: 182 us -> 168 us
    pallas_call x1, Pallas kernels: 182 us -> 168 us  [body(): pl.pallas_call(functools.partial(kernel, EXPERTS, sections), out_shape=[j...]
where the time goes in v3:
time: 171 us
  Pallas kernels  168 us (98%)
  local copies, waits for them, and re-layouts  2.64 us (2%)
    pallas_call x1, Pallas kernels, body(): pl.pallas_call(functools.partial(kernel, EXPERTS, sections), out_shape=[j...  168 us

profile of v3, /device:TPU:1, one launch (start us, length us, event | category | flops | bytes accessed | tf_op | source)
XLA Modules:
  0.0 171.0 jit_solution(14514769306366206897)
XLA Ops:
  0.6 167.7 %shard_map.113 = (bf16[64,3584]{1,0:T(8,128)(2,1)}, bf16[64,3584]{1,0:T(8,128)(2,1)}) custom-call(bf16[64,3584]{1,0:T(8,128)(2,1)} %bitcast.16, bf16[64,3584]{1,0:T(8,128)(2,1)} %bitcast.17, bf16[1,3584]{1,0:T(2,128)(2,1)} %gain.1, s32[1,64]{1,0:T(1,128)} %bitcast.20, s32[1,64]{1,0:T(1,128)} %bitcast.21, f32[1,64]{1,0:T(1,128)} %bitcast.22, ...), custom_call_target="tpu_custom_call" | custom-call | tf_op jit(solution)/shard_map/pallas_call | solution.py:621
  168.3 0.0 copy-start
  168.3 1.9 %copy.14 = bf16[1,64,3584]{2,1,0:T(8,128)(2,1)} copy(bf16[1,64,3584]{2,1,0:T(8,128)(2,1)} %bitcast.19) | data formatting | bytes 917504
  170.2 0.0 copy-done
  170.2 0.8 copy.15
Async XLA Ops:
  168.3 1.9 %copy-start = (bf16[64,3584]{1,0:T(8,128)(2,1)S(1)}, bf16[64,3584]{1,0:T(8,128)(2,1)}, u32[]{:S(2)}) copy-start(bf16[64,3584]{1,0:T(8,128)(2,1)} %get-tuple-element.5) | copy-start | bytes 1376260

commit v4 on v3

--- a/solution.py
+++ b/solution.py
@@ -61,12 +61,12 @@
     hidden,
     columns,
     returned,
-    spread,
+    leaving,
     final,
     residual,
     notes,
     notes_here,
-    sums,
+    token_notes,
     weight_copy,
     raw_send,
     raw_recv,
@@ -134,18 +134,18 @@
 
     @pl.when(pipe > 0)
     def _():
-        @pl.loop(0, experts)
+        @pl.loop(0, ring)
         def _(k):
-            greet((pipe - 1, k * ring + z))
+            greet((pipe - 1, y * ring + k))
 
     @pl.when(pipe < sections - 1)
     def _():
-        @pl.loop(0, experts)
+        @pl.loop(0, ring)
         def _(k):
-            greet((pipe + 1, k * ring + z))
+            greet((pipe + 1, y * ring + k))
 
     neighbours = jnp.where(pipe > 0, 1, 0) + jnp.where(pipe < sections - 1, 1, 0)
-    greeted = experts - 1 + ring - 1 + experts * neighbours
+    greeted = experts - 1 + ring - 1 + ring * neighbours
 
     weight_copies = (
         pltpu.make_async_copy(gate_w, gate_up.at[:units], weight_copy.at[0]),
@@ -405,136 +405,133 @@
 
     def project(g):
         hidden_copy_own(g).wait()
+        size, piece = ring * rows, ring * per // 2
+        row, place = iota((size, size), 0), iota((size, size), 1)
+        same = (place // rows == row // per % ring) & (place % per == row % per)
+        same = same & (place // per % experts == row // (ring * per))
         result = dot_t(hidden[g], down[...]).astype(BF16)
-        piece = rows // 2
-        for b in range(ring):
+        result = jnp.dot(one_hot(same), result, preferred_element_type=F32)
+        for k in range(experts):
             first, second = (
-                result[(2 * b + i) * piece : (2 * b + i + 1) * piece] for i in range(2)
+                result[(2 * k + i) * piece : (2 * k + i + 1) * piece] for i in range(2)
             )
-            columns[g, b] = jnp.concatenate([first, second], axis=1)
-        target = returned.at[g, z % 2, z // 2]
-        pltpu.make_async_copy(columns.at[g, z], target, columns_recv.at[g]).start()
-
-        @pl.loop(1, ring)
+            columns[g, k] = jnp.concatenate([first, second], axis=1).astype(BF16)
+        target = returned.at[g, y]
+        pltpu.make_async_copy(columns.at[g, y], target, columns_recv.at[g]).start()
+
+        @pl.loop(1, experts)
         def _(k):
             remote(
-                columns.at[g, lax.rem(z + k, ring)],
+                columns.at[g, lax.rem(y + k, experts)],
                 target,
                 columns_send.at[g],
                 columns_recv.at[g],
-                at_z(k),
+                at_y(k),
             ).start()
 
-    def give_back(g):
-        wait(returned.at[g], columns_recv.at[g])
-        size, piece = slots // 2, rows // 2
-        row, place = iota((size, size), 0), iota((size, size), 1)
-        same = row // per % FOLD == place // piece
-        same = same & (row // SLAB * per + row % per == place % piece)
-        order = one_hot(same)
-        even, odd = (
-            jnp.dot(
-                order,
-                returned[g, i].reshape(size, width),
-                preferred_element_type=F32,
-            )
-            for i in range(2)
-        )
-        cut = width // 2
+    def note_tokens():
+        row = iota((128, 2 * count), 0)
+        for b in range(ring):
+            lanes = slice(b * 2 * count, (b + 1) * 2 * count)
+            note = jnp.where(row == 0, tables[0:1, lanes], tables[1:2, lanes])
+            token_notes[b] = jnp.transpose(note)
+
+    def collect(stream):
+        members = groups_of(stream)
+        for g in members:
+            if streams_of(g)[0] == stream:
+                wait(returned.at[g], columns_recv.at[g])
+        near = ring // 2
+        span = near * per
+        size = len(members) * experts * span
+        parts = [returned[g].reshape(experts * span, 2 * down.shape[0]) for g in members]
+        source = jnp.concatenate(parts, axis=0)
+        row, place = iota((near * count, size), 0), iota((near * count, size), 1)
+        slot_here = place // (experts * span) * per + place % per + members[0] * per
+        expert_here = place // span % experts
         for i in range(2):
-            lanes = slice(i * cut, (i + 1) * cut)
-            joined = jnp.concatenate([even[:, lanes], odd[:, lanes]], axis=1)
-            spread[g, i * size : (i + 1) * size] = joined.astype(BF16)
-        for stream in streams_of(g):
-            send_back(g, stream)
-
-    def send_back(g, stream):
-        index = g - groups_of(stream)[0]
-
+            note = token_notes[i * near : (i + 1) * near, stream * count : (stream + 1) * count]
+            note = note.reshape(near * count, 128)
+            same = (note[:, 0:1] == expert_here.astype(F32)) & (row // count == place // per % near)
+            same = same & (note[:, 1:2] == slot_here.astype(F32))
+            picked = jnp.dot(one_hot(same), source, preferred_element_type=F32)
+            cut = down.shape[0]
+            picked = picked[:, i * cut : (i + 1) * cut]
+            for b in range(near):
+                first, second = (
+                    picked[(2 * b + k) * count // 2 : (2 * b + k + 1) * count // 2]
+                    for k in range(2)
+                )
+                joined = jnp.concatenate([first, second], axis=1)
+                leaving[stream, i * near + b] = joined.astype(BF16)
+
+    def send_back(stream):
         @pl.when(last(stream))
         def _():
             end = 1 - stream
-            target = final.at[end, index, slab(y)]
-            pltpu.make_async_copy(
-                spread.at[g, slab(y)], target, final_recv.at[end, index]
-            ).start()
-
-            @pl.loop(1, experts)
+            target = final.at[end, z]
+            pltpu.make_async_copy(leaving.at[stream, z], target, final_recv.at[end]).start()
+
+            @pl.loop(1, ring)
             def _(k):
                 remote(
-                    spread.at[g, slab(lax.rem(y + k, experts))],
+                    leaving.at[stream, lax.rem(z + k, ring)],
                     target,
-                    final_send.at[stream, index],
-                    final_recv.at[end, index],
-                    at_y(k),
+                    final_send.at[stream],
+                    final_recv.at[end],
+                    at_z(k),
                 ).start()
 
         @pl.when(jnp.logical_not(last(stream)))
         def _():
-            target = final.at[stream, index, slab(y)]
+            target = final.at[stream, z]
             remote(
-                spread.at[g, slab(y)],
+                leaving.at[stream, z],
                 target,
-                final_send_same.at[stream, index],
-                final_recv.at[stream, index],
+                final_send_same.at[stream],
+                final_recv.at[stream],
                 (onward(stream), position),
             ).start()
 
-            @pl.loop(1, experts)
+            @pl.loop(1, ring)
             def _(k):
-                to = lax.rem(y + k, experts)
+                to = lax.rem(z + k, ring)
                 remote(
-                    spread.at[g, slab(to)],
+                    leaving.at[stream, to],
                     target,
-                    final_send.at[stream, index],
-                    final_recv.at[stream, index],
-                    (onward(stream), to * ring + z),
+                    final_send.at[stream],
+                    final_recv.at[stream],
+                    (onward(stream), y * ring + to),
                 ).start()
 
-    def combine(end, index):
-        if index == 0:
-            wait(residual.at[end], residual_recv.at[end])
-            wait(notes_here.at[end], notes_recv.at[end])
-        wait(final.at[end, index], final_recv.at[end, index])
-        place = iota((count, slots), 1)
-        note = notes_here[end]
-        expert, slot, weight = note[:, 0:1], note[:, 1:2], note[:, 2:3]
-        turned = jnp.where(pipe == 0, end == 0, (pipe == sections - 1) & (end == 1))
-        stream = jnp.where(turned, 1 - end, end)
-        inside = place % per + index * per + stream * CAP // per * per
-        chosen = (expert == (place // SLAB).astype(F32)) & (slot == inside.astype(F32))
-        for c in range(FOLD):
-            cut = slice(c * width, (c + 1) * width)
-            picked = jnp.dot(
-                one_hot(chosen & (place // per % FOLD == c)),
-                final[end, index],
-                preferred_element_type=F32,
-            )
-            if index > 0:
-                picked = picked + sums[end, :, cut]
-            if index < len(groups_of(0)) - 1:
-                sums[end, :, cut] = picked
-            else:
-                total = residual[end, :, cut].astype(F32) + weight * picked
-                outs[end][:, cut] = total.astype(BF16)
-
-    normalize(0)
+    def combine(end):
+        wait(residual.at[end], residual_recv.at[end])
+        wait(notes_here.at[end], notes_recv.at[end])
+        wait(final.at[end], final_recv.at[end])
+        piece, size = down.shape[0], count // 2
+        for k in range(ring // 2):
+            cut = slice(2 * k * piece, 2 * (k + 1) * piece)
+            pair = [final[end, 2 * k + i].astype(F32) for i in range(2)]
+            for i in range(2):
+                mine = slice(i * size, (i + 1) * size)
+                lanes = slice(i * piece, (i + 1) * piece)
+                out = jnp.concatenate([part[:, lanes] for part in pair], axis=1)
+                total = residual[end, mine, cut].astype(F32)
+                total = total + notes_here[end, mine, 2:3] * out
+                outs[end][mine, cut] = total.astype(BF16)
+
+    for stream in range(2):
+        normalize(stream)
+    pl.semaphore_wait(barrier, greeted)
+    for part in range(2):
+        raw_stage(part, 0)
     numbers = [number(0)]
     pack(0, numbers)
-    pl.semaphore_wait(barrier, greeted)
-    raw_stage(0, 0)
     dispatch(0)
-    normalize(1)
-    raw_stage(1, 0)
     numbers.append(number(1))
     send_table(numbers)
-    for g in range(1, groups):
-        pack(g, numbers)
-        dispatch(g)
-    for stream in range(2):
-        send_residual(stream)
-    for copy in weight_copies:
-        copy.wait()
+    pack(1, numbers)
+    dispatch(1)
 
     stages = ring // 2
     final_step = 2 * stages + 1
@@ -550,21 +547,33 @@
             hidden_stage(g, step - stages)
         if step == 2 * stages:
             project(g)
-        if step == final_step:
-            give_back(g)
 
     for step in range(1, (groups - 1) * OFFSET + final_step + 2):
         if step <= stages:
             for part in range(2):
                 raw_stage(part, step)
-        if 0 <= step - stages < groups:
-            dispatch_raw(step - stages)
+        if step == stages:
+            for g in range(groups):
+                dispatch_raw(g)
         for g in range(groups):
             if 0 <= step - 1 - g * OFFSET <= final_step:
                 action(g, step - 1 - g * OFFSET)
-    for index in range(len(groups_of(0))):
-        for end in range(2):
-            combine(end, index)
+        if step == stages + groups - 1:
+            note_tokens()
+        for stream in range(2):
+            if step - 1 - groups_of(stream)[-1] * OFFSET == final_step:
+                collect(stream)
+                send_back(stream)
+        if step + 1 < groups:
+            pack(step + 1, numbers)
+            dispatch(step + 1)
+        if step == groups - 1:
+            for stream in range(2):
+                send_residual(stream)
+            for copy in weight_copies:
+                copy.wait()
+    for end in range(2):
+        combine(end)
 
     wait(tables.at[:, : (ring - 1) * 2 * count], table_send)
     for part in range(2):
@@ -580,15 +589,13 @@
                     wait(token_part(g, part, 0), token_send.at[g, part, direction, hop])
             for hop in range(hops(direction, g)):
                 wait(hidden_own.at[g], hidden_send.at[g, direction, hop])
-        wait(columns.at[g, : ring - 1], columns_send.at[g])
+        wait(columns.at[g, : experts - 1], columns_send.at[g])
     for stream in range(2):
-        for index in range(len(groups_of(stream))):
-            wait(spread.at[0, : slots - SLAB], final_send.at[stream, index])
+        wait(leaving.at[stream, : ring - 1], final_send.at[stream])
 
         @pl.when(jnp.logical_not(last(stream)))
         def _(stream=stream):
-            for index in range(len(groups_of(stream))):
-                wait(spread.at[0, :SLAB], final_send_same.at[stream, index])
+            wait(leaving.at[stream, 0], final_send_same.at[stream])
             wait(residual.at[stream], residual_send.at[stream])
             wait(notes.at[stream], notes_send.at[stream])
 
@@ -612,7 +619,6 @@
     ring = depth // piece
     per = SLAB // FOLD
     groups = 2 * CAP // per
-    mine = -(-CAP // per)
     rows, slots, width = EXPERTS * per, EXPERTS * SLAB, depth // FOLD
     half = ring // 2
     dma = pltpu.SemaphoreType.DMA
@@ -637,14 +643,14 @@
             pltpu.VMEM((groups, ring, (FOLD - 1) * rows, width), BF16),
             pltpu.VMEM((groups, ring * rows, units), BF16),
             pltpu.VMEM((groups, ring * rows, hidden_units), BF16),
-            pltpu.VMEM((groups, ring, rows // 2, 2 * piece), BF16),
-            pltpu.VMEM((groups, 2, ring // 2, rows // 2, 2 * piece), BF16),
-            pltpu.VMEM((groups, slots, width), BF16),
-            pltpu.VMEM((2, mine, slots, width), BF16),
+            pltpu.VMEM((groups, EXPERTS, ring * per // 2, 2 * piece), BF16),
+            pltpu.VMEM((groups, EXPERTS, ring * per // 2, 2 * piece), BF16),
+            pltpu.VMEM((2, ring, count // 2, 2 * piece), BF16),
+            pltpu.VMEM((2, ring, count // 2, 2 * piece), BF16),
             pltpu.VMEM((2, count, depth), BF16),
             pltpu.VMEM((2, count, 128), F32),
             pltpu.VMEM((2, count, 128), F32),
-            pltpu.VMEM((2, count, depth), F32),
+            pltpu.VMEM((ring, 2 * count, 128), F32),
             dma((3,)),
             dma((2, 2, half)),
             dma((2, 2, half)),
@@ -661,9 +667,9 @@
             dma((groups,)),
             dma((groups,)),
             dma((groups,)),
-            dma((2, mine)),
-            dma((2, mine)),
-            dma((2, mine)),
+            dma((2,)),
+            dma((2,)),
+            dma((2,)),
             dma((2,)),
             dma((2,)),
             dma((2,)),

time: 171 us -> 164 us (0.959)
  Pallas kernels: 168 us -> 160 us
    pallas_call x1, Pallas kernels: 168 us -> 160 us  [body(): pl.pallas_call(functools.partial(kernel, EXPERTS, sections), out_shape=[j...]
where the time goes in v4:
time: 164 us
  Pallas kernels  160 us (98%)
  local copies, waits for them, and re-layouts  2.64 us (2%)
    pallas_call x1, Pallas kernels, body(): pl.pallas_call(functools.partial(kernel, EXPERTS, sections), out_shape=[j...  160 us

profile of v4, /device:TPU:1, one launch (start us, length us, event | category | flops | bytes accessed | tf_op | source)
XLA Modules:
  0.0 163.6 jit_solution(13933362529701839511)
XLA Ops:
  0.6 160.3 %shard_map.113 = (bf16[64,3584]{1,0:T(8,128)(2,1)}, bf16[64,3584]{1,0:T(8,128)(2,1)}) custom-call(bf16[64,3584]{1,0:T(8,128)(2,1)} %bitcast.16, bf16[64,3584]{1,0:T(8,128)(2,1)} %bitcast.17, bf16[1,3584]{1,0:T(2,128)(2,1)} %gain.1, s32[1,64]{1,0:T(1,128)} %bitcast.20, s32[1,64]{1,0:T(1,128)} %bitcast.21, f32[1,64]{1,0:T(1,128)} %bitcast.22, ...), custom_call_target="tpu_custom_call" | custom-call | tf_op jit(solution)/shard_map/pallas_call | solution.py:627
  160.9 0.0 copy-start
  160.9 1.9 %copy.14 = bf16[1,64,3584]{2,1,0:T(8,128)(2,1)} copy(bf16[1,64,3584]{2,1,0:T(8,128)(2,1)} %bitcast.19) | data formatting | bytes 917504
  162.8 0.0 copy-done
  162.8 0.8 copy.15
Async XLA Ops:
  160.9 1.9 %copy-start = (bf16[64,3584]{1,0:T(8,128)(2,1)S(1)}, bf16[64,3584]{1,0:T(8,128)(2,1)}, u32[]{:S(2)}) copy-start(bf16[64,3584]{1,0:T(8,128)(2,1)} %get-tuple-element.5) | copy-start | bytes 1376260

commit v5 on v4

--- a/solution.py
+++ b/solution.py
@@ -366,16 +366,17 @@
         ).astype(BF16)
 
     def hide(g):
+        size = ring * rows
+        total = jnp.zeros((size, 2 * units), F32)
+        for c in range(1, FOLD):
+            part = tokens[g, :, (c - 1) * rows : c * rows, :].reshape(size, width)
+            total = total + dot_t(part, gate_up[:, c * width : (c + 1) * width])
         wait(landed_raw.at[g], slab_raw_recv.at[g])
-        size = ring * rows
         row, place = iota((size, size), 0), iota((size, size), 1)
         same = (row // rows == place // per % ring) & (row % per == place % per)
         same = same & (row // per % experts == place // (ring * per))
         part = jnp.dot(one_hot(same), landed_raw[g], preferred_element_type=F32)
-        total = dot_t(part.astype(BF16), gate_up[:, :width])
-        for c in range(1, FOLD):
-            part = tokens[g, :, (c - 1) * rows : c * rows, :].reshape(size, width)
-            total = total + dot_t(part, gate_up[:, c * width : (c + 1) * width])
+        total = total + dot_t(part.astype(BF16), gate_up[:, :width])
         hidden_own[g] = (jax.nn.silu(total[:, :units]) * total[:, units:]).astype(BF16)
 
     def hidden_part(g, owner):

time: 164 us -> 162 us (0.988)
  Pallas kernels: 160 us -> 158 us
    pallas_call x1, Pallas kernels: 160 us -> 158 us  [body(): pl.pallas_call(functools.partial(kernel, EXPERTS, sections), out_shape=[j...]
where the time goes in v5:
time: 162 us
  Pallas kernels  158 us (98%)
  local copies, waits for them, and re-layouts  2.64 us (2%)
    pallas_call x1, Pallas kernels, body(): pl.pallas_call(functools.partial(kernel, EXPERTS, sections), out_shape=[j...  158 us

profile of v5, /device:TPU:1, one launch (start us, length us, event | category | flops | bytes accessed | tf_op | source)
XLA Modules:
  0.0 161.7 jit_solution(13596951860831652132)
XLA Ops:
  0.6 158.4 %shard_map.113 = (bf16[64,3584]{1,0:T(8,128)(2,1)}, bf16[64,3584]{1,0:T(8,128)(2,1)}) custom-call(bf16[64,3584]{1,0:T(8,128)(2,1)} %bitcast.16, bf16[64,3584]{1,0:T(8,128)(2,1)} %bitcast.17, bf16[1,3584]{1,0:T(2,128)(2,1)} %gain.1, s32[1,64]{1,0:T(1,128)} %bitcast.20, s32[1,64]{1,0:T(1,128)} %bitcast.21, f32[1,64]{1,0:T(1,128)} %bitcast.22, ...), custom_call_target="tpu_custom_call" | custom-call | tf_op jit(solution)/shard_map/pallas_call | solution.py:628
  159.1 0.0 copy-start
  159.1 1.9 %copy.14 = bf16[1,64,3584]{2,1,0:T(8,128)(2,1)} copy(bf16[1,64,3584]{2,1,0:T(8,128)(2,1)} %bitcast.19) | data formatting | bytes 917504
  161.0 0.0 copy-done
  161.0 0.8 copy.15
Async XLA Ops:
  159.1 1.9 %copy-start = (bf16[64,3584]{1,0:T(8,128)(2,1)S(1)}, bf16[64,3584]{1,0:T(8,128)(2,1)}, u32[]{:S(2)}) copy-start(bf16[64,3584]{1,0:T(8,128)(2,1)} %get-tuple-element.5) | copy-start | bytes 1376260
